TPU v7x, 128 devices: a whole 4x4x4 slice. The times are simulated.
128 devices in a mesh: day: 4 (over x), chan: 32 (over y, z, core).
Axes of the slice: x: 4, y: 4, z: 4, core: 2. Of those that a mesh axis runs over, the one named last changes fastest.
Arguments:
- strain_raw: bfloat16 [8, 4096, 1024], P('day', 'chan'), may hold values from -320 to 320, as said below
- pair_dist: int32 [32, 3], P('chan'), may hold values from -1 to 4, as said below
Outputs:
- stack: float32 [96, 129, 128, 128], P('chan', None, 'day')
Inputs may be any that keep to these rules, and one draw needn't show every extreme that they name: `pair_dist`: each owner's live slots come first and hold distinct distances with c + distance below 32; every owner has at least one live slot and owner 0 has all 3 live, one of them at distance 4. `strain_raw`: channels differ in scale and offset.
All inputs are finite; a program needn't handle non-finite values.
Results may differ from a plain program's by a relative error of at most 0.0039.
Values may be sent and summed in bfloat16 or wider, within the bound.
No kernel may reach another device: no remote copies, remote signals or barrier semaphores. Data moves between devices by JAX's collectives and lax.ppermute only.
A program may use at most 256 MiB of HBM per device.

v0:
```python
import functools
import jax
import jax.numpy as jnp
from jax import lax
from jax.experimental import pallas as pl
from jax.experimental.pallas import tpu as pltpu
from jax.sharding import PartitionSpec as P

BW = 128
SAMPLES = 1024
MAXLAG = 64
REACH = 4
TILES_DEV = 3
LAGS = 2 * MAXLAG + 1
SHIFTS = MAXLAG + 1
GROUP = 13
GROUPS = SHIFTS // GROUP
BF = jnp.bfloat16


def whiten_kernel(raw_ref, out_ref):
    values = raw_ref[...].astype(jnp.float32)
    centred = values - jnp.mean(values, axis=-1, keepdims=True)
    spread = jnp.mean(centred * centred, axis=-1, keepdims=True)
    out_ref[...] = (centred * lax.rsqrt(spread + 1e-06)).astype(BF)


def whiten(strain_raw):
    return pl.pallas_call(
        whiten_kernel,
        in_specs=[pl.BlockSpec(memory_space=pltpu.VMEM)],
        out_specs=pl.BlockSpec(memory_space=pltpu.VMEM),
        out_shape=jax.ShapeDtypeStruct(strain_raw.shape, BF),
        cost_estimate=pl.CostEstimate(
            flops=8 * strain_raw.size, bytes_accessed=4 * strain_raw.size, transcendentals=0
        ),
        name="whiten",
    )(strain_raw)


def gather_kernel(moves, flag, *refs):
    arrays, outs, sems = refs[: moves[0]], refs[moves[0] : -1], refs[-1]
    for parity in (0, 1):

        @pl.when(flag[0] == parity)
        def _():
            copies = [
                pltpu.make_async_copy(
                    arrays[i].at[pl.ds(at, n)], outs[j].at[pl.ds(to, n)], sems.at[c]
                )
                for c, (i, at, j, to, n) in enumerate(moves[1 + parity])
            ]
            for copy in copies:
                copy.start()
            for copy in copies:
                copy.wait()


def gather(flag, arrays, counts, even, odd, name):
    any_spec = pl.BlockSpec(memory_space=pl.ANY)
    shape = arrays[0].shape[1:]
    return pl.pallas_call(
        functools.partial(gather_kernel, (len(arrays), even, odd)),
        grid_spec=pltpu.PrefetchScalarGridSpec(
            num_scalar_prefetch=1,
            grid=(1,),
            in_specs=[any_spec] * len(arrays),
            out_specs=[any_spec] * len(counts),
            scratch_shapes=[pltpu.SemaphoreType.DMA((max(len(even), len(odd)),))],
        ),
        out_shape=[jax.ShapeDtypeStruct((n,) + shape, BF) for n in counts],
        name=name,
    )(flag, *arrays)


def correlate_kernel(places, operands, reach, part, norm, win, *refs):
    sets = len(places)
    first = part == "all"
    arrays, refs = refs[:operands], refs[operands:]
    if not first:
        refs = refs[1:]
    out_ref, araw, braw, tiles, before, *refs = refs
    lefts, rights, refs = refs[:sets], refs[sets : 2 * sets], refs[2 * sets :]
    shifted, sums, sems = refs[: -sets - 3], refs[-sets - 3 : -4], refs[-4:]
    sem_a, sem_b, sem_in, sem_out = sems
    days, rows = araw.shape[1:3]
    slots = tiles.shape[0]
    row0 = pl.multiple_of(win[0] * rows, rows)

    lives, found = [], jnp.bool_(False)
    for k in range(TILES_DEV):
        dist = win[1 + k]
        plain = jnp.logical_and(dist >= 0, dist % 2 == 0)
        head = jnp.logical_and(plain, jnp.logical_not(found))
        found = jnp.logical_or(found, plain)
        if part == "all":
            lives.append(dist >= 0)
        elif part == "head":
            lives.append(head)
        else:
            lives.append(jnp.logical_and(dist >= 0, jnp.logical_not(head)))
    seats = [jnp.int32(0)]
    for k in range(TILES_DEV):
        seats.append(seats[-1] + lives[k].astype(jnp.int32))

    def copy_in(k, seat):
        return pltpu.make_async_copy(out_ref.at[k], before.at[seat], sem_in.at[seat])

    def copy_out(k, seat):
        return pltpu.make_async_copy(tiles.at[seat], out_ref.at[k], sem_out.at[seat])

    def copy_zero(k):
        return pltpu.make_async_copy(before, out_ref.at[k], sem_in.at[k])

    def copy_left(s):
        array, start = places[s][0]
        return pltpu.make_async_copy(
            arrays[array].at[pl.ds(start, days), pl.ds(row0, rows), :], araw.at[s], sem_a.at[s]
        )

    def copy_right(s, seat, n):
        array, start = places[s][1 + n]
        return pltpu.make_async_copy(
            arrays[array].at[pl.ds(start, days)], braw.at[seat, s], sem_b.at[seat, s]
        )

    @pl.when(seats[-1] > 0)
    def _():
        for s in range(sets):
            copy_left(s).start()
        for k in range(TILES_DEV):
            for n, e in enumerate(reach):

                @pl.when(jnp.logical_and(lives[k], win[1 + k] == e))
                def _():
                    for s in range(sets):
                        copy_right(s, seats[k], n).start()

            if not first:

                @pl.when(lives[k])
                def _():
                    copy_in(k, seats[k]).start()

        if first:
            before[...] = jnp.zeros(before.shape, jnp.float32)
            for k in range(TILES_DEV):
                pl.when(jnp.logical_not(lives[k]))(copy_zero(k).start)

        gap = jnp.zeros((rows, MAXLAG), BF)
        gap_b = jnp.zeros((BW, MAXLAG), BF)
        for s in range(sets):
            copy_left(s).wait()
            lefts[s][...] = jnp.concatenate(
                [p for d in range(days) for p in (araw[s, d], gap)], 1
            )

        def make_shift(s, g):
            for i in range(GROUP):
                shift = g * GROUP + i
                value = lefts[s][...]
                if shift:
                    value = pltpu.roll(value, shift, 1)
                shifted[(s * GROUPS + g) % len(shifted)][i * rows : (i + 1) * rows, :] = value

        def make_right(s, seat):
            rights[s][0:BW, :] = jnp.concatenate(
                [p for d in range(days) for p in (gap_b, braw[seat, s, d])], 1
            )
            rights[s][BW : 2 * BW, :] = jnp.concatenate(
                [p for d in range(days) for p in (braw[seat, s, d], gap_b)], 1
            )

        def one_slot(k, seat, with_shift):
            pltpu.make_async_copy(braw.at[seat, 0], braw.at[seat, 0], sem_b.at[seat, 0]).wait()
            make_right(0, seat)
            if with_shift:
                make_shift(0, 0)
            for s in range(sets):
                if s == 1:
                    for r in range(1, sets):
                        pltpu.make_async_copy(
                            braw.at[seat, r], braw.at[seat, r], sem_b.at[seat, r]
                        ).wait()
                        make_right(r, seat)
                    copy_in(k, seat).wait()
                for g in range(GROUPS):
                    if with_shift and g + 1 < GROUPS:
                        make_shift(s, g + 1)
                    elif with_shift and s + 1 < sets:
                        make_shift(s + 1, 0)
                    product = lax.dot_general(
                        shifted[(s * GROUPS + g) % len(shifted)][...],
                        rights[s][...],
                        (((1,), (1,)), ((), ())),
                        preferred_element_type=jnp.float32,
                    )
                    kept = GROUP - (g == GROUPS - 1)
                    for half, count, lag in (
                        (0, kept, g * GROUP),
                        (1, GROUP, MAXLAG + g * GROUP),
                    ):
                        value = product[:, half * BW : (half + 1) * BW].reshape(GROUP, rows, BW)
                        value = value[:count]
                        at = pl.ds(lag, count)
                        if s:
                            value = value + sums[s - 1][at]
                        if s + 1 < sets:
                            sums[s][at] = value
                        elif first:
                            tiles[seat, at] = value * norm
                        else:
                            tiles[seat, at] = value * norm + before[seat, at]
            copy_out(k, seat).start()

        def loop(k, seat):
            hit = lives[0]
            for n in range(1, TILES_DEV):
                hit = jnp.where(k == n, lives[n], hit)

            @pl.when(jnp.logical_and(hit, seat == 0))
            def _():
                one_slot(k, seat, True)

            if slots > 1:

                @pl.when(jnp.logical_and(hit, seat > 0))
                def _():
                    one_slot(k, seat, False)

            return seat + hit.astype(jnp.int32)

        lax.fori_loop(0, TILES_DEV, loop, jnp.int32(0))

    for k in range(TILES_DEV):
        pl.when(lives[k])(copy_out(k, seats[k]).wait)
        if first:
            pl.when(jnp.logical_not(lives[k]))(copy_zero(k).wait)


def correlate(sets, reach, part, slots, scalars, total, rows, norm, name):
    count = len(sets)
    days = 2
    span = days * (SAMPLES + MAXLAG)
    operands = []

    def place(block):
        array, start = block
        for i, other in enumerate(operands):
            if other is array:
                return i, start
        operands.append(array)
        return len(operands) - 1, start

    places = [
        [place(own)] + [place(partners[e]) for e in reach] for own, partners in sets
    ]
    arrays = len(operands)
    first = part == "all"
    aliases = {}
    if not first:
        aliases = {1 + len(operands): 0}
        operands.append(total)
    tile = (TILES_DEV, LAGS, rows, BW)
    any_spec = pl.BlockSpec(memory_space=pl.ANY)
    flops = 4 * count * slots * SHIFTS * rows * BW * span
    return pl.pallas_call(
        functools.partial(correlate_kernel, places, arrays, reach, part, norm),
        grid_spec=pltpu.PrefetchScalarGridSpec(
            num_scalar_prefetch=1,
            grid=(1,),
            in_specs=[any_spec] * len(operands),
            out_specs=any_spec,
            scratch_shapes=[
                pltpu.VMEM((count, days, rows, SAMPLES), BF),
                pltpu.VMEM((slots, count, days, BW, SAMPLES), BF),
                pltpu.VMEM((slots,) + tile[1:], jnp.float32),
                pltpu.VMEM(tile[1:] if first else (slots,) + tile[1:], jnp.float32),
            ]
            + [pltpu.VMEM((rows, span), BF)] * count
            + [pltpu.VMEM((2 * BW, span), BF)] * count
            + [pltpu.VMEM((GROUP * rows, span), BF)] * (GROUPS * count if slots > 1 else 2)
            + [pltpu.VMEM(tile[1:], jnp.float32)] * (count - 1)
            + [
                pltpu.SemaphoreType.DMA((count,)),
                pltpu.SemaphoreType.DMA((slots, count)),
                pltpu.SemaphoreType.DMA((TILES_DEV,)),
                pltpu.SemaphoreType.DMA((TILES_DEV,)),
            ],
        ),
        out_shape=jax.ShapeDtypeStruct(tile, jnp.float32),
        input_output_aliases=aliases,
        compiler_params=pltpu.CompilerParams(vmem_limit_bytes=(50 if count * slots > 3 else 30) << 20),
        cost_estimate=pl.CostEstimate(
            flops=flops, bytes_accessed=8 << 20, transcendentals=0
        ),
        name=name,
    )(scalars, *operands)


def moved(array, axis, by):
    devices = lax.axis_size(axis)
    if axis == "day":
        pairs = [(i, (i + by) % devices) for i in range(devices)]
    else:
        pairs = [(i, i + by) for i in range(devices) if 0 <= i + by < devices]
    return lax.ppermute(array, axis, pairs)


def swapped(array):
    devices = lax.axis_size("chan")
    return lax.ppermute(array, "chan", [(i, i ^ 1) for i in range(devices)])


def local(strain_raw, pair_dist):
    day = lax.axis_index("day")
    even = lax.axis_index("chan") % 2 == 0
    rows = BW // lax.axis_size("day")
    total_days = strain_raw.shape[0] * lax.axis_size("day")
    norm = float((SAMPLES * total_days) ** -0.5)
    scalars = jnp.concatenate([day.astype(jnp.int32)[None], pair_dist[0].astype(jnp.int32)])

    own = whiten(strain_raw)
    tie = lax.optimization_barrier
    parity = (lax.axis_index("chan") % 2).astype(jnp.int32)[None]

    z2, z4 = moved(own, "chan", -2), moved(own, "chan", -4)
    own_p, own_m, own_2 = (moved(own, "day", by) for by in (1, -1, 2))
    z2, z4, own_p, own_m, own_2 = tie((z2, z4, own_p, own_m, own_2))

    z2_2, z4_2 = moved(own_2, "chan", -2), moved(own_2, "chan", -4)
    both = [(1, 0, 0, 0, 2), (2, 0, 0, 2, 2)]
    zz, mine = gather(
        parity,
        (own, z2, z4),
        (4, 4),
        both + [(1, 0, 1, 0, 2), (2, 0, 1, 2, 2)],
        both + [(0, 0, 1, 0, 2), (1, 0, 1, 2, 2)],
        "pair_near",
    )
    zz_p, zz_m = moved(zz, "day", 1), moved(zz, "day", -1)
    pair = swapped(mine)
    near = ((own, 0), {0: (own, 0), 1: (pair, 0), 2: (z2, 0), 3: (pair, 2), 4: (z4, 0)})
    tiles = correlate([near], (0, 1, 2, 3, 4), "all", 3, scalars, None, rows, norm, "near_days")
    zz_p, zz_m, z2_2, z4_2, tiles = tie((zz_p, zz_m, z2_2, z4_2, tiles))

    (mine,) = gather(
        parity,
        (own_p, own_m, own_2, zz_p, zz_m, z2_2, z4_2),
        (12,),
        [(3, 0, 0, 0, 4), (4, 0, 0, 4, 4), (5, 0, 0, 8, 2), (6, 0, 0, 10, 2)],
        [
            (0, 0, 0, 0, 2),
            (3, 0, 0, 2, 2),
            (1, 0, 0, 4, 2),
            (4, 0, 0, 6, 2),
            (2, 0, 0, 8, 2),
            (5, 0, 0, 10, 2),
        ],
        "pair_far",
    )
    pair = swapped(mine)
    owns = (own_p, own_m, own_2)
    twos = ((zz_p, 0), (zz_m, 0), (z2_2, 0))
    fours = ((zz_p, 2), (zz_m, 2), (z4_2, 0))
    sets = [((owns[i], 0), {0: (owns[i], 0), 2: twos[i], 4: fours[i]}) for i in range(3)]
    tiles = correlate(sets, (0, 2, 4), "head", 1, scalars, tiles, rows, norm, "far_days_one")
    sets = [
        (
            (owns[i], 0),
            {
                0: (owns[i], 0),
                1: (pair, 4 * i),
                2: twos[i],
                3: (pair, 4 * i + 2),
                4: fours[i],
            },
        )
        for i in range(3)
    ]
    return correlate(sets, (0, 1, 2, 3, 4), "rest", 2, scalars, tiles, rows, norm, "far_days_rest")


def solution(mesh):
    placed = (P("day", "chan", None), P("chan", None))
    return jax.shard_map(
        local, mesh=mesh, in_specs=placed, out_specs=P("chan", None, "day", None), check_vma=False
    )
```

profile of v0, /device:TPU:15, one launch (start us, length us, event | category | flops | bytes accessed | tf_op | source)
XLA Modules:
  0.0 277.9 jit_solution(8542668350533981983)
XLA Ops:
  0.0 2.2 whiten.1.refs_0_
  2.2 1.1 collective-permute-start.4
  3.3 0.0 collective-permute-start.3
  3.3 2.7 collective-permute-start.2
  6.0 5.4 %collective-permute-start.1 = (bf16[2,128,1024]{2,1,0:T(8,128)(2,1)}, bf16[2,128,1024]{2,1,0:T(8,128)(2,1)S(1)}, u32[]{:S(2)}, u32[]{:S(2)}) collective-permute-start(bf16[2,128,1024]{2,1,0:T(8,128)(2,1)} %whiten.1.refs_0_), channel_id=1, source_target_pairs={{4,0},{5,1},{6,2},{7,3},{8,4},{9,5},{10,6},{11,7},{12,8},{13,9},{1... | collective-permute-start | bytes 1572872 | tf_op jit(solution)/shard_map/ppermute | solution.py:307
  11.4 2.3 collective-permute-start
  13.7 3.0 %collective-permute-done.4.refs_2_.refs_4_.refs_5_ = bf16[2,128,1024]{2,1,0:T(8,128)(2,1)S(1)} collective-permute-done((bf16[2,128,1024]{2,1,0:T(8,128)(2,1)}, bf16[2,128,1024]{2,1,0:T(8,128)(2,1)S(1)}, u32[]{:S(2)}, u32[]{:S(2)}) %collective-permute-start.4) | collective-permute-done | bytes 524320 | tf_op jit(solution)/shard_map/ppermute | solution.py:307
  16.7 12.2 %collective-permute-done.3.refs_1_.refs_2_.refs_3_ = bf16[2,128,1024]{2,1,0:T(8,128)(2,1)S(1)} collective-permute-done((bf16[2,128,1024]{2,1,0:T(8,128)(2,1)}, bf16[2,128,1024]{2,1,0:T(8,128)(2,1)S(1)}, u32[]{:S(2)}, u32[]{:S(2)}) %collective-permute-start.3) | collective-permute-done | bytes 524320 | tf_op jit(solution)/shard_map/ppermute | solution.py:307
  29.0 0.0 collective-permute-done.2.refs_0_
  29.0 0.0 collective-permute-done.1.refs_2_.refs_3_
  29.0 7.9 %collective-permute-done.refs_1_.refs_2_ = bf16[2,128,1024]{2,1,0:T(8,128)(2,1)S(1)} collective-permute-done((bf16[2,128,1024]{2,1,0:T(8,128)(2,1)}, bf16[2,128,1024]{2,1,0:T(8,128)(2,1)S(1)}, u32[]{:S(2)}, u32[]{:S(2)}) %collective-permute-start) | collective-permute-done | bytes 524320 | tf_op jit(solution)/shard_map/ppermute | solution.py:307
  36.9 0.0 copy-done.20
  36.9 0.8 copy-done.22
  37.7 64.7 %pair_near.1 = (bf16[4,128,1024]{2,1,0:T(8,128)(2,1)}, bf16[4,128,1024]{2,1,0:T(8,128)(2,1)}) custom-call(s32[1]{0:T(128)} %bitcast.2.flag, bf16[2,128,1024]{2,1,0:T(8,128)(2,1)} %whiten.1.refs_0_, bf16[2,128,1024]{2,1,0:T(8,128)(2,1)} %copy-done.22, bf16[2,128,1024]{2,1,0:T(8,128)(2,1)} %copy-done.20), custom_call_target="tpu_custom_call" | custom-call | tf_op jit(solution)/shard_map/pair_near/pallas_call | solution.py:62
  102.4 0.6 collective-permute-start.9
  103.0 0.0 collective-permute-start.6
  103.0 2.7 collective-permute-start.5
  105.6 0.7 pad_add_fusion.win
  106.4 1.9 collective-permute-start.8
  108.3 4.3 %collective-permute-start.7 = (bf16[2,128,1024]{2,1,0:T(8,128)(2,1)S(1)}, bf16[2,128,1024]{2,1,0:T(8,128)(2,1)S(1)}, u32[]{:S(2)}, u32[]{:S(2)}) collective-permute-start(bf16[2,128,1024]{2,1,0:T(8,128)(2,1)S(1)} %collective-permute-done.4.refs_2_.refs_4_.refs_5_), channel_id=1, source_target_pairs={{2,0},{3,1},{4,2},{5,3},{6,4},{7,5},{8,6},{9,7},{10,8},{11,9},{12,... | collective-permute-start | bytes 1572872 | tf_op jit(solution)/shard_map/ppermute | solution.py:307
  112.6 0.0 collective-permute-done.9.refs_1_
  112.6 0.0 copy-start
  112.6 1.0 copy-done
  113.6 1.0 copy-done.21
  114.7 1.0 copy-done.23
  115.7 11.5 %near_days.1.refs_7_ = f32[3,129,32,128]{3,2,1,0:T(8,128)} custom-call(s32[4]{0:T(128)S(1)} %pad_add_fusion.win, bf16[2,128,1024]{2,1,0:T(8,128)(2,1)S(1)} %copy-done, bf16[4,128,1024]{2,1,0:T(8,128)(2,1)} %collective-permute-done.9.refs_1_, bf16[2,128,1024]{2,1,0:T(8,128)(2,1)S(1)} %copy-done.23, bf16[2,128,1024]{2,1,0:T(8,128)(2,1)S(1)} %copy-done.21), custom_call_target="tpu_custom_call" | custom-call | flops 6952058880 | bytes 8388608 | tf_op jit(solution)/shard_map/near_days/pallas_call | solution.py:267
  127.3 0.0 collective-permute-done.8.refs_6_.refs_7_
  127.3 8.6 %collective-permute-done.7.refs_5_.refs_6_ = bf16[2,128,1024]{2,1,0:T(8,128)(2,1)S(1)} collective-permute-done((bf16[2,128,1024]{2,1,0:T(8,128)(2,1)S(1)}, bf16[2,128,1024]{2,1,0:T(8,128)(2,1)S(1)}, u32[]{:S(2)}, u32[]{:S(2)}) %collective-permute-start.7) | collective-permute-done | bytes 524320 | tf_op jit(solution)/shard_map/ppermute | solution.py:307
  135.8 0.0 collective-permute-done.6.refs_4_.refs_3_
  135.9 0.8 copy-done.17
  136.6 0.0 collective-permute-done.5.refs_3_.refs_1_.refs_2_
  136.6 1.0 copy-done.1
  137.6 1.0 copy-done.3
  138.6 96.4 %pair_far.1 = bf16[12,128,1024]{2,1,0:T(8,128)(2,1)} custom-call(s32[1]{0:T(128)} %bitcast.2.flag, bf16[2,128,1024]{2,1,0:T(8,128)(2,1)} %copy-done.11, bf16[2,128,1024]{2,1,0:T(8,128)(2,1)} %copy-done.9, bf16[2,128,1024]{2,1,0:T(8,128)(2,1)} %copy-done.6, bf16[4,128,1024]{2,1,0:T(8,128)(2,1)} %copy-done.3, bf16[4,128,1024]{2,1,0:T(8,128)(2,1)} %copy-done.1, ...), custom_call_target="tpu_custom_call" | custom-call | tf_op jit(solution)/shard_map/pair_far/pallas_call | solution.py:62
  235.1 0.6 collective-permute-start.10
  235.6 0.0 copy-done.10
  235.7 1.2 copy-done.2
  236.9 1.2 copy-done.4
  238.1 1.0 copy-done.7
  239.1 1.0 copy-done.12
  240.2 1.0 copy-done.15
  241.2 1.0 copy-done.18
  242.3 0.0 copy-start.19
  242.3 13.1 %far_days_one.1.refs_8_ = f32[3,129,32,128]{3,2,1,0:T(8,128)} custom-call(s32[4]{0:T(128)S(1)} %pad_add_fusion.win, bf16[2,128,1024]{2,1,0:T(8,128)(2,1)S(1)} %copy-done.12, bf16[4,128,1024]{2,1,0:T(8,128)(2,1)S(1)} %copy-done.4, bf16[2,128,1024]{2,1,0:T(8,128)(2,1)S(1)} %copy-done.10, ...), custom_call_target="tpu_custom_call", output_to_operand_aliasing={{}: (8, {})} | custom-call | flops 6952058880 | bytes 8388608 | tf_op jit(solution)/shard_map/far_days_one/pallas_call | solution.py:267
  255.4 0.0 collective-permute-done.10.refs_1_
  255.4 1.6 copy-done.24
  257.1 0.0 copy-done.8
  257.1 20.6 %far_days_rest.1 = f32[3,129,32,128]{3,2,1,0:T(8,128)} custom-call(s32[4]{0:T(128)S(1)} %pad_add_fusion.win, bf16[2,128,1024]{2,1,0:T(8,128)(2,1)S(1)} %copy-done.13, bf16[12,128,1024]{2,1,0:T(8,128)(2,1)} %copy-done.24, bf16[4,128,1024]{2,1,0:T(8,128)(2,1)S(1)} %copy-done.5, bf16[2,128,1024]{2,1,0:T(8,128)(2,1)S(1)} %copy-done.10, ...), custom_call_target="tpu_custom_call", output_to_operand_aliasing={{}: (9, {})} | custom-call | flops 13904117760 | bytes 8388608 | tf_op jit(solution)/shard_map/far_days_rest/pallas_call | solution.py:267
  (31 shorter events, 0.1 us)
Async XLA Ops:
  2.2 14.6 %collective-permute-start.4 = (bf16[2,128,1024]{2,1,0:T(8,128)(2,1)}, bf16[2,128,1024]{2,1,0:T(8,128)(2,1)S(1)}, u32[]{:S(2)}, u32[]{:S(2)}) collective-permute-start(bf16[2,128,1024]{2,1,0:T(8,128)(2,1)} %whiten.1.refs_0_), channel_id=1, source_target_pairs={{0,64},{32,96},{64,0},{96,32},{1,65},{33,97},{65,1},{97,33},{2,66}... | collective-permute-start | bytes 1572872 | tf_op jit(solution)/shard_map/ppermute | solution.py:307
  3.3 25.7 %collective-permute-start.3 = (bf16[2,128,1024]{2,1,0:T(8,128)(2,1)}, bf16[2,128,1024]{2,1,0:T(8,128)(2,1)S(1)}, u32[]{:S(2)}, u32[]{:S(2)}) collective-permute-start(bf16[2,128,1024]{2,1,0:T(8,128)(2,1)} %whiten.1.refs_0_), channel_id=1, source_target_pairs={{0,96},{32,0},{64,32},{96,64},{1,97},{33,1},{65,33},{97,65},{2,98}... | collective-permute-start | bytes 1572872 | tf_op jit(solution)/shard_map/ppermute | solution.py:307
  3.3 25.7 %collective-permute-start.2 = (bf16[2,128,1024]{2,1,0:T(8,128)(2,1)}, bf16[2,128,1024]{2,1,0:T(8,128)(2,1)S(1)}, u32[]{:S(2)}, u32[]{:S(2)}) collective-permute-start(bf16[2,128,1024]{2,1,0:T(8,128)(2,1)} %whiten.1.refs_0_), channel_id=1, source_target_pairs={{0,32},{32,64},{64,96},{96,0},{1,33},{33,65},{65,97},{97,1},{2,34}... | collective-permute-start | bytes 1572872 | tf_op jit(solution)/shard_map/ppermute | solution.py:307
  6.0 23.0 %collective-permute-start.1 = (bf16[2,128,1024]{2,1,0:T(8,128)(2,1)}, bf16[2,128,1024]{2,1,0:T(8,128)(2,1)S(1)}, u32[]{:S(2)}, u32[]{:S(2)}) collective-permute-start(bf16[2,128,1024]{2,1,0:T(8,128)(2,1)} %whiten.1.refs_0_), channel_id=1, source_target_pairs={{4,0},{5,1},{6,2},{7,3},{8,4},{9,5},{10,6},{11,7},{12,8},{13,9},{1... | collective-permute-start | bytes 1572872 | tf_op jit(solution)/shard_map/ppermute | solution.py:307
  11.4 25.6 %collective-permute-start = (bf16[2,128,1024]{2,1,0:T(8,128)(2,1)}, bf16[2,128,1024]{2,1,0:T(8,128)(2,1)S(1)}, u32[]{:S(2)}, u32[]{:S(2)}) collective-permute-start(bf16[2,128,1024]{2,1,0:T(8,128)(2,1)} %whiten.1.refs_0_), channel_id=1, source_target_pairs={{2,0},{3,1},{4,2},{5,3},{6,4},{7,5},{8,6},{9,7},{10,8},{11,9},{12,... | collective-permute-start | bytes 1572872 | tf_op jit(solution)/shard_map/ppermute | solution.py:307
  16.7 119.9 %copy-start.6 = (bf16[2,128,1024]{2,1,0:T(8,128)(2,1)}, bf16[2,128,1024]{2,1,0:T(8,128)(2,1)S(1)}, u32[]{:S(2)}) copy-start(bf16[2,128,1024]{2,1,0:T(8,128)(2,1)S(1)} %collective-permute-done.4.refs_2_.refs_4_.refs_5_) | copy-start | bytes 1572868
  29.0 98.3 %copy-start.9 = (bf16[2,128,1024]{2,1,0:T(8,128)(2,1)}, bf16[2,128,1024]{2,1,0:T(8,128)(2,1)S(1)}, u32[]{:S(2)}) copy-start(bf16[2,128,1024]{2,1,0:T(8,128)(2,1)S(1)} %collective-permute-done.3.refs_1_.refs_2_.refs_3_) | copy-start | bytes 1572868
  29.0 74.0 %copy-start.11 = (bf16[2,128,1024]{2,1,0:T(8,128)(2,1)}, bf16[2,128,1024]{2,1,0:T(8,128)(2,1)S(1)}, u32[]{:S(2)}) copy-start(bf16[2,128,1024]{2,1,0:T(8,128)(2,1)S(1)} %collective-permute-done.2.refs_0_) | copy-start | bytes 1572868
  29.0 7.9 %copy-start.20 = (bf16[2,128,1024]{2,1,0:T(8,128)(2,1)}, bf16[2,128,1024]{2,1,0:T(8,128)(2,1)S(1)}, u32[]{:S(2)}) copy-start(bf16[2,128,1024]{2,1,0:T(8,128)(2,1)S(1)} %collective-permute-done.1.refs_2_.refs_3_) | copy-start | bytes 1572868
  36.9 0.8 copy-start.22
  102.4 10.2 %collective-permute-start.9 = (bf16[4,128,1024]{2,1,0:T(8,128)(2,1)}, bf16[4,128,1024]{2,1,0:T(8,128)(2,1)}, u32[]{:S(2)}, u32[]{:S(2)}) collective-permute-start(bf16[4,128,1024]{2,1,0:T(8,128)(2,1)} %get-tuple-element.23), channel_id=1, source_target_pairs={{0,1},{1,0},{2,3},{3,2},{4,5},{5,4},{6,7},{7,6},{8,9},{9,8},{10,11... | collective-permute-start | bytes 3145736 | tf_op jit(solution)/shard_map/ppermute | solution.py:312
  103.0 32.9 %collective-permute-start.6 = (bf16[4,128,1024]{2,1,0:T(8,128)(2,1)}, bf16[4,128,1024]{2,1,0:T(8,128)(2,1)S(1)}, u32[]{:S(2)}, u32[]{:S(2)}) collective-permute-start(bf16[4,128,1024]{2,1,0:T(8,128)(2,1)} %get-tuple-element.22), channel_id=1, source_target_pairs={{0,96},{32,0},{64,32},{96,64},{1,97},{33,1},{65,33},{97,65},{2,98}... | collective-permute-start | bytes 3145736 | tf_op jit(solution)/shard_map/ppermute | solution.py:307
  103.0 33.7 %collective-permute-start.5 = (bf16[4,128,1024]{2,1,0:T(8,128)(2,1)}, bf16[4,128,1024]{2,1,0:T(8,128)(2,1)S(1)}, u32[]{:S(2)}, u32[]{:S(2)}) collective-permute-start(bf16[4,128,1024]{2,1,0:T(8,128)(2,1)} %get-tuple-element.22), channel_id=1, source_target_pairs={{0,32},{32,64},{64,96},{96,0},{1,33},{33,65},{65,97},{97,1},{2,34}... | collective-permute-start | bytes 3145736 | tf_op jit(solution)/shard_map/ppermute | solution.py:307
  106.4 20.9 %collective-permute-start.8 = (bf16[2,128,1024]{2,1,0:T(8,128)(2,1)S(1)}, bf16[2,128,1024]{2,1,0:T(8,128)(2,1)S(1)}, u32[]{:S(2)}, u32[]{:S(2)}) collective-permute-start(bf16[2,128,1024]{2,1,0:T(8,128)(2,1)S(1)} %collective-permute-done.4.refs_2_.refs_4_.refs_5_), channel_id=1, source_target_pairs={{4,0},{5,1},{6,2},{7,3},{8,4},{9,5},{10,6},{11,7},{12,8},{13,9},{1... | collective-permute-start | bytes 1572872 | tf_op jit(solution)/shard_map/ppermute | solution.py:307
  108.3 27.5 %collective-permute-start.7 = (bf16[2,128,1024]{2,1,0:T(8,128)(2,1)S(1)}, bf16[2,128,1024]{2,1,0:T(8,128)(2,1)S(1)}, u32[]{:S(2)}, u32[]{:S(2)}) collective-permute-start(bf16[2,128,1024]{2,1,0:T(8,128)(2,1)S(1)} %collective-permute-done.4.refs_2_.refs_4_.refs_5_), channel_id=1, source_target_pairs={{2,0},{3,1},{4,2},{5,3},{6,4},{7,5},{8,6},{9,7},{10,8},{11,9},{12,... | collective-permute-start | bytes 1572872 | tf_op jit(solution)/shard_map/ppermute | solution.py:307
  112.6 1.0 copy-start
  113.6 1.0 copy-start.21
  114.7 1.0 copy-start.23
  127.3 8.6 %copy-start.14 = (bf16[2,128,1024]{2,1,0:T(8,128)(2,1)}, bf16[2,128,1024]{2,1,0:T(8,128)(2,1)S(1)}, u32[]{:S(2)}) copy-start(bf16[2,128,1024]{2,1,0:T(8,128)(2,1)S(1)} %collective-permute-done.8.refs_6_.refs_7_) | copy-start | bytes 1572868
  127.3 108.4 %copy-start.10 = (bf16[2,128,1024]{2,1,0:T(8,128)(2,1)S(1)}, bf16[2,128,1024]{2,1,0:T(8,128)(2,1)}, u32[]{:S(2)}) copy-start(bf16[2,128,1024]{2,1,0:T(8,128)(2,1)} %copy-done.9) | copy-start | bytes 1572868
  135.8 0.8 copy-start.17
  136.6 1.0 copy-start.1
  137.6 1.0 copy-start.3
  235.1 20.3 %collective-permute-start.10 = (bf16[12,128,1024]{2,1,0:T(8,128)(2,1)}, bf16[12,128,1024]{2,1,0:T(8,128)(2,1)S(1)}, u32[]{:S(2)}, u32[]{:S(2)}) collective-permute-start(bf16[12,128,1024]{2,1,0:T(8,128)(2,1)} %pair_far.1), channel_id=1, source_target_pairs={{0,1},{1,0},{2,3},{3,2},{4,5},{5,4},{6,7},{7,6},{8,9},{9,8},{10,11... | collective-permute-start | bytes 9437192 | tf_op jit(solution)/shard_map/ppermute | solution.py:312
  235.7 1.2 copy-start.2
  236.9 1.2 copy-start.4
  238.1 1.0 copy-start.7
  239.1 1.0 copy-start.12
  240.2 1.0 copy-start.15
  241.2 1.0 copy-start.18
  242.3 14.8 %copy-start.5 = (bf16[4,128,1024]{2,1,0:T(8,128)(2,1)S(1)}, bf16[4,128,1024]{2,1,0:T(8,128)(2,1)}, u32[]{:S(2)}) copy-start(bf16[4,128,1024]{2,1,0:T(8,128)(2,1)} %copy-done.3) | copy-start | bytes 3145732
  242.3 14.8 %copy-start.8 = (bf16[2,128,1024]{2,1,0:T(8,128)(2,1)S(1)}, bf16[2,128,1024]{2,1,0:T(8,128)(2,1)}, u32[]{:S(2)}) copy-start(bf16[2,128,1024]{2,1,0:T(8,128)(2,1)} %copy-done.6) | copy-start | bytes 1572868
  242.3 14.8 %copy-start.13 = (bf16[2,128,1024]{2,1,0:T(8,128)(2,1)S(1)}, bf16[2,128,1024]{2,1,0:T(8,128)(2,1)}, u32[]{:S(2)}) copy-start(bf16[2,128,1024]{2,1,0:T(8,128)(2,1)} %copy-done.11) | copy-start | bytes 1572868
  242.3 14.8 %copy-start.16 = (bf16[2,128,1024]{2,1,0:T(8,128)(2,1)S(1)}, bf16[2,128,1024]{2,1,0:T(8,128)(2,1)}, u32[]{:S(2)}) copy-start(bf16[2,128,1024]{2,1,0:T(8,128)(2,1)} %copy-done.14) | copy-start | bytes 1572868
  242.3 14.8 %copy-start.19 = (bf16[2,128,1024]{2,1,0:T(8,128)(2,1)S(1)}, bf16[2,128,1024]{2,1,0:T(8,128)(2,1)}, u32[]{:S(2)}) copy-start(bf16[2,128,1024]{2,1,0:T(8,128)(2,1)} %copy-done.17) | copy-start | bytes 1572868
  255.4 1.6 copy-start.24
where the time goes:
time: 279 us; the launch traced here: 278 us
  Pallas kernels  208 us (75%)
  waiting for transfers between devices  31.7 us (11%)
  starting transfers between devices  21.6 us (8%)
  local copies, waits for them, and re-layouts  14.9 us (5%)
    pallas_call x2, Pallas kernels, gather(): pl.pallas_call(functools.partial(gather_kernel, (len(arrays), even, odd))...  161 us
    pallas_call x3, Pallas kernels, correlate(): pl.pallas_call(functools.partial(correlate_kernel, places, arrays, reach,...  45.2 us
    ppermute x9, waiting for transfers between devices, moved(): return lax.ppermute(array, axis, pairs)  31.7 us
    ppermute x9, starting transfers between devices, moved(): return lax.ppermute(array, axis, pairs)  20.4 us
    unnamed x50, local copies, waits for them, and re-layouts  14.9 us
  transfers between devices with their start and end apart: 11, of which 4 were waited for; matrix products, arithmetic and copies ran while one was open for 0% of the time, Pallas kernels for 9%

commit v1 on v0

--- a/solution.py
+++ b/solution.py
@@ -57,23 +57,21 @@
 
 
 def gather(flag, arrays, counts, even, odd, name):
+    vmem_spec = pl.BlockSpec(memory_space=pltpu.VMEM)
     any_spec = pl.BlockSpec(memory_space=pl.ANY)
     shape = arrays[0].shape[1:]
     return pl.pallas_call(
         functools.partial(gather_kernel, (len(arrays), even, odd)),
-        grid_spec=pltpu.PrefetchScalarGridSpec(
-            num_scalar_prefetch=1,
-            grid=(1,),
-            in_specs=[any_spec] * len(arrays),
-            out_specs=[any_spec] * len(counts),
-            scratch_shapes=[pltpu.SemaphoreType.DMA((max(len(even), len(odd)),))],
-        ),
+        in_specs=[pl.BlockSpec(memory_space=pltpu.SMEM)] + [any_spec] * len(arrays),
+        out_specs=[vmem_spec] * len(counts),
         out_shape=[jax.ShapeDtypeStruct((n,) + shape, BF) for n in counts],
+        scratch_shapes=[pltpu.SemaphoreType.DMA((max(len(even), len(odd)),))],
+        compiler_params=pltpu.CompilerParams(vmem_limit_bytes=16 << 20),
         name=name,
     )(flag, *arrays)
 
 
-def correlate_kernel(places, operands, reach, part, norm, win, *refs):
+def correlate_kernel(places, operands, part, norm, win, *refs):
     sets = len(places)
     first = part == "all"
     arrays, refs = refs[:operands], refs[operands:]
@@ -81,7 +79,7 @@
         refs = refs[1:]
     out_ref, araw, braw, tiles, before, *refs = refs
     lefts, rights, refs = refs[:sets], refs[sets : 2 * sets], refs[2 * sets :]
-    shifted, sums, sems = refs[: -sets - 3], refs[-sets - 3 : -4], refs[-4:]
+    shifted, sums, sems = refs[: 1 - sets - 4], refs[1 - sets - 4 : -4], refs[-4:]
     sem_a, sem_b, sem_in, sem_out = sems
     days, rows = araw.shape[1:3]
     slots = tiles.shape[0]
@@ -129,12 +127,12 @@
         for s in range(sets):
             copy_left(s).start()
         for k in range(TILES_DEV):
-            for n, e in enumerate(reach):
+            for e in range(0, REACH + 1, 2 if part == "head" else 1):
 
                 @pl.when(jnp.logical_and(lives[k], win[1 + k] == e))
                 def _():
                     for s in range(sets):
-                        copy_right(s, seats[k], n).start()
+                        copy_right(s, seats[k], e).start()
 
             if not first:
 
@@ -171,66 +169,51 @@
                 [p for d in range(days) for p in (braw[seat, s, d], gap_b)], 1
             )
 
-        def one_slot(k, seat, with_shift):
-            pltpu.make_async_copy(braw.at[seat, 0], braw.at[seat, 0], sem_b.at[seat, 0]).wait()
-            make_right(0, seat)
+        def work(seat, with_shift):
+            for s in range(sets):
+                copy_right(s, seat, 0).wait()
+                make_right(s, seat)
+            if not first:
+                copy_in(0, seat).wait()
             if with_shift:
                 make_shift(0, 0)
-            for s in range(sets):
-                if s == 1:
-                    for r in range(1, sets):
-                        pltpu.make_async_copy(
-                            braw.at[seat, r], braw.at[seat, r], sem_b.at[seat, r]
-                        ).wait()
-                        make_right(r, seat)
-                    copy_in(k, seat).wait()
-                for g in range(GROUPS):
-                    if with_shift and g + 1 < GROUPS:
-                        make_shift(s, g + 1)
-                    elif with_shift and s + 1 < sets:
-                        make_shift(s + 1, 0)
-                    product = lax.dot_general(
-                        shifted[(s * GROUPS + g) % len(shifted)][...],
-                        rights[s][...],
-                        (((1,), (1,)), ((), ())),
-                        preferred_element_type=jnp.float32,
-                    )
-                    kept = GROUP - (g == GROUPS - 1)
-                    for half, count, lag in (
-                        (0, kept, g * GROUP),
-                        (1, GROUP, MAXLAG + g * GROUP),
-                    ):
-                        value = product[:, half * BW : (half + 1) * BW].reshape(GROUP, rows, BW)
-                        value = value[:count]
-                        at = pl.ds(lag, count)
-                        if s:
-                            value = value + sums[s - 1][at]
-                        if s + 1 < sets:
-                            sums[s][at] = value
-                        elif first:
-                            tiles[seat, at] = value * norm
-                        else:
-                            tiles[seat, at] = value * norm + before[seat, at]
-            copy_out(k, seat).start()
-
-        def loop(k, seat):
-            hit = lives[0]
-            for n in range(1, TILES_DEV):
-                hit = jnp.where(k == n, lives[n], hit)
-
-            @pl.when(jnp.logical_and(hit, seat == 0))
-            def _():
-                one_slot(k, seat, True)
-
+            for n in range(sets * GROUPS):
+                s, g = divmod(n, GROUPS)
+                if with_shift and n + 1 < sets * GROUPS:
+                    make_shift(*divmod(n + 1, GROUPS))
+                product = lax.dot_general(
+                    shifted[n % len(shifted)][...],
+                    rights[s][...],
+                    (((1,), (1,)), ((), ())),
+                    preferred_element_type=jnp.float32,
+                )
+                kept = GROUP - (g == GROUPS - 1)
+                for half, count, lag in (
+                    (0, kept, g * GROUP),
+                    (1, GROUP, MAXLAG + g * GROUP),
+                ):
+                    value = product[:, half * BW : (half + 1) * BW]
+                    value = value.reshape(GROUP, rows, BW)[:count]
+                    at = pl.ds(lag, count)
+                    if s:
+                        value = value + sums[s - 1][at]
+                    if s + 1 < sets:
+                        sums[s][at] = value
+                    elif first:
+                        tiles[seat, at] = value * norm
+                    else:
+                        tiles[seat, at] = value * norm + before[seat, at]
+
+        def loop(seat, carry):
+            pl.when(seat == 0)(functools.partial(work, seat, True))
             if slots > 1:
-
-                @pl.when(jnp.logical_and(hit, seat > 0))
-                def _():
-                    one_slot(k, seat, False)
-
-            return seat + hit.astype(jnp.int32)
-
-        lax.fori_loop(0, TILES_DEV, loop, jnp.int32(0))
+                pl.when(seat > 0)(functools.partial(work, seat, False))
+            for k in range(TILES_DEV):
+                mine = jnp.logical_and(lives[k], seats[k] == seat)
+                pl.when(mine)(copy_out(k, seat).start)
+            return carry
+
+        lax.fori_loop(0, seats[-1], loop, 0)
 
     for k in range(TILES_DEV):
         pl.when(lives[k])(copy_out(k, seats[k]).wait)
@@ -238,7 +221,7 @@
             pl.when(jnp.logical_not(lives[k]))(copy_zero(k).wait)
 
 
-def correlate(sets, reach, part, slots, scalars, total, rows, norm, name):
+def correlate(sets, part, slots, scalars, total, rows, norm, name):
     count = len(sets)
     days = 2
     span = days * (SAMPLES + MAXLAG)
@@ -253,7 +236,7 @@
         return len(operands) - 1, start
 
     places = [
-        [place(own)] + [place(partners[e]) for e in reach] for own, partners in sets
+        [place(own)] + [place(partners.get(e, own)) for e in range(REACH + 1)] for own, partners in sets
     ]
     arrays = len(operands)
     first = part == "all"
@@ -262,10 +245,9 @@
         aliases = {1 + len(operands): 0}
         operands.append(total)
     tile = (TILES_DEV, LAGS, rows, BW)
-    any_spec = pl.BlockSpec(memory_space=pl.ANY)
-    flops = 4 * count * slots * SHIFTS * rows * BW * span
+    any_spec = pl.BlockSpec(memory_space=pltpu.HBM)
     return pl.pallas_call(
-        functools.partial(correlate_kernel, places, arrays, reach, part, norm),
+        functools.partial(correlate_kernel, places, arrays, part, norm),
         grid_spec=pltpu.PrefetchScalarGridSpec(
             num_scalar_prefetch=1,
             grid=(1,),
@@ -290,9 +272,9 @@
         ),
         out_shape=jax.ShapeDtypeStruct(tile, jnp.float32),
         input_output_aliases=aliases,
-        compiler_params=pltpu.CompilerParams(vmem_limit_bytes=(50 if count * slots > 3 else 30) << 20),
+        compiler_params=pltpu.CompilerParams(vmem_limit_bytes=(46 if slots * count > 3 else 32) << 20),
         cost_estimate=pl.CostEstimate(
-            flops=flops, bytes_accessed=8 << 20, transcendentals=0
+            flops=1 << 20, bytes_accessed=1 << 16, transcendentals=0
         ),
         name=name,
     )(scalars, *operands)
@@ -324,9 +306,9 @@
     tie = lax.optimization_barrier
     parity = (lax.axis_index("chan") % 2).astype(jnp.int32)[None]
 
+    own_p, own_m, own_2 = (moved(own, "day", by) for by in (1, -1, 2))
     z2, z4 = moved(own, "chan", -2), moved(own, "chan", -4)
-    own_p, own_m, own_2 = (moved(own, "day", by) for by in (1, -1, 2))
-    z2, z4, own_p, own_m, own_2 = tie((z2, z4, own_p, own_m, own_2))
+    own_p, own_m, own_2, z2, z4 = tie((own_p, own_m, own_2, z2, z4))
 
     z2_2, z4_2 = moved(own_2, "chan", -2), moved(own_2, "chan", -4)
     both = [(1, 0, 0, 0, 2), (2, 0, 0, 2, 2)]
@@ -341,7 +323,7 @@
     zz_p, zz_m = moved(zz, "day", 1), moved(zz, "day", -1)
     pair = swapped(mine)
     near = ((own, 0), {0: (own, 0), 1: (pair, 0), 2: (z2, 0), 3: (pair, 2), 4: (z4, 0)})
-    tiles = correlate([near], (0, 1, 2, 3, 4), "all", 3, scalars, None, rows, norm, "near_days")
+    tiles = correlate([near], "all", 3, scalars, None, rows, norm, "near_days")
     zz_p, zz_m, z2_2, z4_2, tiles = tie((zz_p, zz_m, z2_2, z4_2, tiles))
 
     (mine,) = gather(
@@ -364,21 +346,12 @@
     twos = ((zz_p, 0), (zz_m, 0), (z2_2, 0))
     fours = ((zz_p, 2), (zz_m, 2), (z4_2, 0))
     sets = [((owns[i], 0), {0: (owns[i], 0), 2: twos[i], 4: fours[i]}) for i in range(3)]
-    tiles = correlate(sets, (0, 2, 4), "head", 1, scalars, tiles, rows, norm, "far_days_one")
+    tiles = correlate(sets, "head", 1, scalars, tiles, rows, norm, "far_days_one")
     sets = [
-        (
-            (owns[i], 0),
-            {
-                0: (owns[i], 0),
-                1: (pair, 4 * i),
-                2: twos[i],
-                3: (pair, 4 * i + 2),
-                4: fours[i],
-            },
-        )
-        for i in range(3)
+        (own, {**blocks, 1: (pair, 4 * i), 3: (pair, 4 * i + 2)})
+        for i, (own, blocks) in enumerate(sets)
     ]
-    return correlate(sets, (0, 1, 2, 3, 4), "rest", 2, scalars, tiles, rows, norm, "far_days_rest")
+    return correlate(sets, "rest", 2, scalars, tiles, rows, norm, "far_days_rest")
 
 
 def solution(mesh):

time: 279 us -> 106 us (0.38)
  the two profiles are of different devices: /device:TPU:15 before, /device:TPU:23 now
where the time goes in v1:
time: 106 us; the launch traced here: 105 us
  Pallas kernels  48.7 us (46%)
  waiting for transfers between devices  28.1 us (27%)
  starting transfers between devices  22.7 us (21%)
  local copies, waits for them, and re-layouts  4.37 us (4%)
    pallas_call x3, Pallas kernels, correlate(): pl.pallas_call(functools.partial(correlate_kernel, places, arrays, part,...  43.8 us
    ppermute x9, waiting for transfers between devices, moved(): return lax.ppermute(array, axis, pairs)  28.1 us
    ppermute x9, starting transfers between devices, moved(): return lax.ppermute(array, axis, pairs)  21.5 us
    unnamed x16, local copies, waits for them, and re-layouts  4.37 us
    pallas_call x2, Pallas kernels, gather(): pl.pallas_call(functools.partial(gather_kernel, (len(arrays), even, odd))...  2.79 us
    pallas_call x1, Pallas kernels, whiten(): pl.pallas_call(whiten_kernel, in_specs=[pl.BlockSpec(memory_space=pltpu.V...  2.17 us
  transfers between devices with their start and end apart: 11, of which 4 were waited for; matrix products, arithmetic and copies ran while one was open for 1% of the time, Pallas kernels for 23%

profile of v1, /device:TPU:23, one launch (start us, length us, event | category | flops | bytes accessed | tf_op | source)
XLA Modules:
  0.0 105.0 jit_solution(12492182338361074276)
XLA Ops:
  0.0 2.2 %whiten.1.refs_0_ = bf16[2,128,1024]{2,1,0:T(8,128)(2,1)} custom-call(bf16[2,128,1024]{2,1,0:T(8,128)(2,1)} %raw_ref.1), custom_call_target="tpu_custom_call" | custom-call | flops 2097152 | bytes 1048576 | tf_op jit(solution)/shard_map/whiten/pallas_call | solution.py:29
  2.2 5.4 %collective-permute-start.4 = (bf16[2,128,1024]{2,1,0:T(8,128)(2,1)}, bf16[2,128,1024]{2,1,0:T(8,128)(2,1)S(1)}, u32[]{:S(2)}, u32[]{:S(2)}) collective-permute-start(bf16[2,128,1024]{2,1,0:T(8,128)(2,1)} %whiten.1.refs_0_), channel_id=1, source_target_pairs={{4,0},{5,1},{6,2},{7,3},{8,4},{9,5},{10,6},{11,7},{12,8},{13,9},{1... | collective-permute-start | bytes 1572872 | tf_op jit(solution)/shard_map/ppermute | solution.py:289
  7.6 2.3 %collective-permute-start.3 = (bf16[2,128,1024]{2,1,0:T(8,128)(2,1)}, bf16[2,128,1024]{2,1,0:T(8,128)(2,1)S(1)}, u32[]{:S(2)}, u32[]{:S(2)}) collective-permute-start(bf16[2,128,1024]{2,1,0:T(8,128)(2,1)} %whiten.1.refs_0_), channel_id=1, source_target_pairs={{2,0},{3,1},{4,2},{5,3},{6,4},{7,5},{8,6},{9,7},{10,8},{11,9},{12,... | collective-permute-start | bytes 1572872 | tf_op jit(solution)/shard_map/ppermute | solution.py:289
  9.9 1.2 %collective-permute-start.2 = (bf16[2,128,1024]{2,1,0:T(8,128)(2,1)}, bf16[2,128,1024]{2,1,0:T(8,128)(2,1)S(1)}, u32[]{:S(2)}, u32[]{:S(2)}) collective-permute-start(bf16[2,128,1024]{2,1,0:T(8,128)(2,1)} %whiten.1.refs_0_), channel_id=1, source_target_pairs={{0,64},{32,96},{64,0},{96,32},{1,65},{33,97},{65,1},{97,33},{2,66}... | collective-permute-start | bytes 1572872 | tf_op jit(solution)/shard_map/ppermute | solution.py:289
  11.1 0.0 collective-permute-start.1
  11.1 2.7 %collective-permute-start = (bf16[2,128,1024]{2,1,0:T(8,128)(2,1)}, bf16[2,128,1024]{2,1,0:T(8,128)(2,1)S(1)}, u32[]{:S(2)}, u32[]{:S(2)}) collective-permute-start(bf16[2,128,1024]{2,1,0:T(8,128)(2,1)} %whiten.1.refs_0_), channel_id=1, source_target_pairs={{0,32},{32,64},{64,96},{96,0},{1,33},{33,65},{65,97},{97,1},{2,34}... | collective-permute-start | bytes 1572872 | tf_op jit(solution)/shard_map/ppermute | solution.py:289
  13.8 5.7 %collective-permute-done.4.refs_2_.refs_3_ = bf16[2,128,1024]{2,1,0:T(8,128)(2,1)S(1)} collective-permute-done((bf16[2,128,1024]{2,1,0:T(8,128)(2,1)}, bf16[2,128,1024]{2,1,0:T(8,128)(2,1)S(1)}, u32[]{:S(2)}, u32[]{:S(2)}) %collective-permute-start.4) | collective-permute-done | bytes 524320 | tf_op jit(solution)/shard_map/ppermute | solution.py:289
  19.5 0.0 copy-start.4
  19.5 13.6 %collective-permute-done.3.refs_1_.refs_2_ = bf16[2,128,1024]{2,1,0:T(8,128)(2,1)S(1)} collective-permute-done((bf16[2,128,1024]{2,1,0:T(8,128)(2,1)}, bf16[2,128,1024]{2,1,0:T(8,128)(2,1)S(1)}, u32[]{:S(2)}, u32[]{:S(2)}) %collective-permute-start.3) | collective-permute-done | bytes 524320 | tf_op jit(solution)/shard_map/ppermute | solution.py:289
  33.1 0.0 copy-start.6
  33.1 0.0 collective-permute-done.2.refs_2_.refs_4_.refs_5_
  33.1 3.7 %collective-permute-done.1.refs_1_.refs_2_.refs_3_ = bf16[2,128,1024]{2,1,0:T(8,128)(2,1)S(1)} collective-permute-done((bf16[2,128,1024]{2,1,0:T(8,128)(2,1)}, bf16[2,128,1024]{2,1,0:T(8,128)(2,1)S(1)}, u32[]{:S(2)}, u32[]{:S(2)}) %collective-permute-start.1) | collective-permute-done | bytes 524320 | tf_op jit(solution)/shard_map/ppermute | solution.py:289
  36.8 0.0 collective-permute-done.refs_0_
  36.8 0.0 copy-start
  36.8 0.0 copy-start.2
  36.8 1.2 %copy-done.2 = bf16[2,128,1024]{2,1,0:T(8,128)(2,1)S(1)} copy-done((bf16[2,128,1024]{2,1,0:T(8,128)(2,1)S(1)}, bf16[2,128,1024]{2,1,0:T(8,128)(2,1)}, u32[]{:S(2)}) %copy-start.2) | copy-done | bytes 524312
  38.0 1.5 %pair_near.1 = (bf16[4,128,1024]{2,1,0:T(8,128)(2,1)}, bf16[4,128,1024]{2,1,0:T(8,128)(2,1)}) custom-call(s32[1]{0:T(128)} %bitcast.2.flag, bf16[2,128,1024]{2,1,0:T(8,128)(2,1)S(1)} %copy-done.2, bf16[2,128,1024]{2,1,0:T(8,128)(2,1)S(1)} %collective-permute-done.3.refs_1_.refs_2_, bf16[2,128,1024]{2,1,0:T(8,128)(2,1)S(1)} %collective-permute-done.4.refs_2_.refs_3_), custom_call_target="tpu_custom_call" | custom-call | tf_op jit(solution)/shard_map/pair_near/pallas_call | solution.py:63
  39.5 0.6 collective-permute-start.9
  40.1 0.0 copy-done.4
  40.1 0.0 copy-done
  40.1 0.0 copy-done.6
  40.1 0.6 collective-permute-start.6
  40.7 2.1 %collective-permute-start.5 = (bf16[4,128,1024]{2,1,0:T(8,128)(2,1)}, bf16[4,128,1024]{2,1,0:T(8,128)(2,1)S(1)}, u32[]{:S(2)}, u32[]{:S(2)}) collective-permute-start(bf16[4,128,1024]{2,1,0:T(8,128)(2,1)} %get-tuple-element.22), channel_id=1, source_target_pairs={{0,32},{32,64},{64,96},{96,0},{1,33},{33,65},{65,97},{97,1},{2,34}... | collective-permute-start | bytes 3145736 | tf_op jit(solution)/shard_map/ppermute | solution.py:289
  42.9 3.9 %collective-permute-start.8 = (bf16[2,128,1024]{2,1,0:T(8,128)(2,1)S(1)}, bf16[2,128,1024]{2,1,0:T(8,128)(2,1)}, u32[]{:S(2)}, u32[]{:S(2)}) collective-permute-start(bf16[2,128,1024]{2,1,0:T(8,128)(2,1)S(1)} %collective-permute-done.2.refs_2_.refs_4_.refs_5_), channel_id=1, source_target_pairs={{4,0},{5,1},{6,2},{7,3},{8,4},{9,5},{10,6},{11,7},{12,8},{13,9},{1... | collective-permute-start | bytes 1572872 | tf_op jit(solution)/shard_map/ppermute | solution.py:289
  46.7 3.2 %collective-permute-start.7 = (bf16[2,128,1024]{2,1,0:T(8,128)(2,1)S(1)}, bf16[2,128,1024]{2,1,0:T(8,128)(2,1)}, u32[]{:S(2)}, u32[]{:S(2)}) collective-permute-start(bf16[2,128,1024]{2,1,0:T(8,128)(2,1)S(1)} %collective-permute-done.2.refs_2_.refs_4_.refs_5_), channel_id=1, source_target_pairs={{2,0},{3,1},{4,2},{5,3},{6,4},{7,5},{8,6},{9,7},{10,8},{11,9},{12,... | collective-permute-start | bytes 1572872 | tf_op jit(solution)/shard_map/ppermute | solution.py:289
  50.0 0.0 copy-start.1
  50.0 0.8 pad_add_fusion.win
  50.8 0.0 collective-permute-done.9.refs_1_
  50.8 0.0 copy-start.3
  50.8 1.0 copy-done.3
  51.8 0.0 copy-start.5
  51.8 1.0 copy-done.5
  52.9 0.0 copy-start.7
  52.9 1.0 copy-done.7
  53.9 11.5 %near_days.1.refs_7_ = f32[3,129,32,128]{3,2,1,0:T(8,128)} custom-call(s32[4]{0:T(128)S(1)} %pad_add_fusion.win, bf16[2,128,1024]{2,1,0:T(8,128)(2,1)S(1)} %copy-done.3, bf16[4,128,1024]{2,1,0:T(8,128)(2,1)} %collective-permute-done.9.refs_1_, bf16[2,128,1024]{2,1,0:T(8,128)(2,1)S(1)} %copy-done.7, bf16[2,128,1024]{2,1,0:T(8,128)(2,1)S(1)} %copy-done.5), custom_call_target="tpu_custom_call" | custom-call | flops 1048576 | bytes 65536 | tf_op jit(solution)/shard_map/near_days/pallas_call | solution.py:249
  65.4 0.0 collective-permute-done.8.refs_6_.refs_7_
  65.4 5.1 %collective-permute-done.7.refs_5_.refs_6_ = bf16[2,128,1024]{2,1,0:T(8,128)(2,1)} collective-permute-done((bf16[2,128,1024]{2,1,0:T(8,128)(2,1)S(1)}, bf16[2,128,1024]{2,1,0:T(8,128)(2,1)}, u32[]{:S(2)}, u32[]{:S(2)}) %collective-permute-start.7) | collective-permute-done | bytes 524320 | tf_op jit(solution)/shard_map/ppermute | solution.py:289
  70.5 0.0 collective-permute-done.6.refs_4_.refs_3_
  70.5 0.0 collective-permute-done.5.refs_3_.refs_1_.refs_2_
  70.5 0.0 copy-done.1
  70.5 1.3 %pair_far.1 = bf16[12,128,1024]{2,1,0:T(8,128)(2,1)S(1)} custom-call(s32[1]{0:T(128)} %bitcast.2.flag, bf16[2,128,1024]{2,1,0:T(8,128)(2,1)S(1)} %copy-done.1, bf16[2,128,1024]{2,1,0:T(8,128)(2,1)S(1)} %collective-permute-done.1.refs_1_.refs_2_.refs_3_, bf16[2,128,1024]{2,1,0:T(8,128)(2,1)S(1)} %collective-permute-done.2.refs_2_.refs_4_.refs_5_, ...), custom_call_target="tpu_custom_call" | custom-call | tf_op jit(solution)/shard_map/pair_far/pallas_call | solution.py:63
  71.8 0.7 collective-permute-start.10
  72.5 12.2 %far_days_one.1.refs_8_ = f32[3,129,32,128]{3,2,1,0:T(8,128)} custom-call(s32[4]{0:T(128)S(1)} %pad_add_fusion.win, bf16[2,128,1024]{2,1,0:T(8,128)(2,1)S(1)} %copy-done.1, bf16[4,128,1024]{2,1,0:T(8,128)(2,1)S(1)} %collective-permute-done.5.refs_3_.refs_1_.refs_2_, ...), custom_call_target="tpu_custom_call", output_to_operand_aliasing={{}: (8, {})} | custom-call | flops 1048576 | bytes 65536 | tf_op jit(solution)/shard_map/far_days_one/pallas_call | solution.py:249
  84.7 0.0 collective-permute-done.10.refs_1_
  84.7 20.1 %far_days_rest.1 = f32[3,129,32,128]{3,2,1,0:T(8,128)} custom-call(s32[4]{0:T(128)S(1)} %pad_add_fusion.win, bf16[2,128,1024]{2,1,0:T(8,128)(2,1)S(1)} %copy-done.1, bf16[12,128,1024]{2,1,0:T(8,128)(2,1)S(1)} %collective-permute-done.10.refs_1_, ...), custom_call_target="tpu_custom_call", output_to_operand_aliasing={{}: (9, {})} | custom-call | flops 1048576 | bytes 65536 | tf_op jit(solution)/shard_map/far_days_rest/pallas_call | solution.py:249
Async XLA Ops:
  2.2 17.3 %collective-permute-start.4 = (bf16[2,128,1024]{2,1,0:T(8,128)(2,1)}, bf16[2,128,1024]{2,1,0:T(8,128)(2,1)S(1)}, u32[]{:S(2)}, u32[]{:S(2)}) collective-permute-start(bf16[2,128,1024]{2,1,0:T(8,128)(2,1)} %whiten.1.refs_0_), channel_id=1, source_target_pairs={{4,0},{5,1},{6,2},{7,3},{8,4},{9,5},{10,6},{11,7},{12,8},{13,9},{1... | collective-permute-start | bytes 1572872 | tf_op jit(solution)/shard_map/ppermute | solution.py:289
  7.6 25.6 %collective-permute-start.3 = (bf16[2,128,1024]{2,1,0:T(8,128)(2,1)}, bf16[2,128,1024]{2,1,0:T(8,128)(2,1)S(1)}, u32[]{:S(2)}, u32[]{:S(2)}) collective-permute-start(bf16[2,128,1024]{2,1,0:T(8,128)(2,1)} %whiten.1.refs_0_), channel_id=1, source_target_pairs={{2,0},{3,1},{4,2},{5,3},{6,4},{7,5},{8,6},{9,7},{10,8},{11,9},{12,... | collective-permute-start | bytes 1572872 | tf_op jit(solution)/shard_map/ppermute | solution.py:289
  9.9 23.2 %collective-permute-start.2 = (bf16[2,128,1024]{2,1,0:T(8,128)(2,1)}, bf16[2,128,1024]{2,1,0:T(8,128)(2,1)S(1)}, u32[]{:S(2)}, u32[]{:S(2)}) collective-permute-start(bf16[2,128,1024]{2,1,0:T(8,128)(2,1)} %whiten.1.refs_0_), channel_id=1, source_target_pairs={{0,64},{32,96},{64,0},{96,32},{1,65},{33,97},{65,1},{97,33},{2,66}... | collective-permute-start | bytes 1572872 | tf_op jit(solution)/shard_map/ppermute | solution.py:289
  11.1 25.7 %collective-permute-start.1 = (bf16[2,128,1024]{2,1,0:T(8,128)(2,1)}, bf16[2,128,1024]{2,1,0:T(8,128)(2,1)S(1)}, u32[]{:S(2)}, u32[]{:S(2)}) collective-permute-start(bf16[2,128,1024]{2,1,0:T(8,128)(2,1)} %whiten.1.refs_0_), channel_id=1, source_target_pairs={{0,96},{32,0},{64,32},{96,64},{1,97},{33,1},{65,33},{97,65},{2,98}... | collective-permute-start | bytes 1572872 | tf_op jit(solution)/shard_map/ppermute | solution.py:289
  11.1 25.7 %collective-permute-start = (bf16[2,128,1024]{2,1,0:T(8,128)(2,1)}, bf16[2,128,1024]{2,1,0:T(8,128)(2,1)S(1)}, u32[]{:S(2)}, u32[]{:S(2)}) collective-permute-start(bf16[2,128,1024]{2,1,0:T(8,128)(2,1)} %whiten.1.refs_0_), channel_id=1, source_target_pairs={{0,32},{32,64},{64,96},{96,0},{1,33},{33,65},{65,97},{97,1},{2,34}... | collective-permute-start | bytes 1572872 | tf_op jit(solution)/shard_map/ppermute | solution.py:289
  19.5 20.6 %copy-start.4 = (bf16[2,128,1024]{2,1,0:T(8,128)(2,1)}, bf16[2,128,1024]{2,1,0:T(8,128)(2,1)S(1)}, u32[]{:S(2)}) copy-start(bf16[2,128,1024]{2,1,0:T(8,128)(2,1)S(1)} %collective-permute-done.4.refs_2_.refs_3_) | copy-start | bytes 1572868
  33.1 7.0 %copy-start.6 = (bf16[2,128,1024]{2,1,0:T(8,128)(2,1)}, bf16[2,128,1024]{2,1,0:T(8,128)(2,1)S(1)}, u32[]{:S(2)}) copy-start(bf16[2,128,1024]{2,1,0:T(8,128)(2,1)S(1)} %collective-permute-done.3.refs_1_.refs_2_) | copy-start | bytes 1572868
  36.8 3.3 %copy-start = (bf16[2,128,1024]{2,1,0:T(8,128)(2,1)}, bf16[2,128,1024]{2,1,0:T(8,128)(2,1)S(1)}, u32[]{:S(2)}) copy-start(bf16[2,128,1024]{2,1,0:T(8,128)(2,1)S(1)} %collective-permute-done.refs_0_) | copy-start | bytes 1572868
  36.8 1.2 %copy-start.2 = (bf16[2,128,1024]{2,1,0:T(8,128)(2,1)S(1)}, bf16[2,128,1024]{2,1,0:T(8,128)(2,1)}, u32[]{:S(2)}) copy-start(bf16[2,128,1024]{2,1,0:T(8,128)(2,1)} %whiten.1.refs_0_) | copy-start | bytes 1572868
  39.5 11.3 %collective-permute-start.9 = (bf16[4,128,1024]{2,1,0:T(8,128)(2,1)}, bf16[4,128,1024]{2,1,0:T(8,128)(2,1)}, u32[]{:S(2)}, u32[]{:S(2)}) collective-permute-start(bf16[4,128,1024]{2,1,0:T(8,128)(2,1)} %get-tuple-element.23), channel_id=1, source_target_pairs={{0,1},{1,0},{2,3},{3,2},{4,5},{5,4},{6,7},{7,6},{8,9},{9,8},{10,11... | collective-permute-start | bytes 3145736 | tf_op jit(solution)/shard_map/ppermute | solution.py:294
  40.1 30.4 %collective-permute-start.6 = (bf16[4,128,1024]{2,1,0:T(8,128)(2,1)}, bf16[4,128,1024]{2,1,0:T(8,128)(2,1)S(1)}, u32[]{:S(2)}, u32[]{:S(2)}) collective-permute-start(bf16[4,128,1024]{2,1,0:T(8,128)(2,1)} %get-tuple-element.22), channel_id=1, source_target_pairs={{0,96},{32,0},{64,32},{96,64},{1,97},{33,1},{65,33},{97,65},{2,98}... | collective-permute-start | bytes 3145736 | tf_op jit(solution)/shard_map/ppermute | solution.py:289
  40.7 29.8 %collective-permute-start.5 = (bf16[4,128,1024]{2,1,0:T(8,128)(2,1)}, bf16[4,128,1024]{2,1,0:T(8,128)(2,1)S(1)}, u32[]{:S(2)}, u32[]{:S(2)}) collective-permute-start(bf16[4,128,1024]{2,1,0:T(8,128)(2,1)} %get-tuple-element.22), channel_id=1, source_target_pairs={{0,32},{32,64},{64,96},{96,0},{1,33},{33,65},{65,97},{97,1},{2,34}... | collective-permute-start | bytes 3145736 | tf_op jit(solution)/shard_map/ppermute | solution.py:289
  42.9 22.6 %collective-permute-start.8 = (bf16[2,128,1024]{2,1,0:T(8,128)(2,1)S(1)}, bf16[2,128,1024]{2,1,0:T(8,128)(2,1)}, u32[]{:S(2)}, u32[]{:S(2)}) collective-permute-start(bf16[2,128,1024]{2,1,0:T(8,128)(2,1)S(1)} %collective-permute-done.2.refs_2_.refs_4_.refs_5_), channel_id=1, source_target_pairs={{4,0},{5,1},{6,2},{7,3},{8,4},{9,5},{10,6},{11,7},{12,8},{13,9},{1... | collective-permute-start | bytes 1572872 | tf_op jit(solution)/shard_map/ppermute | solution.py:289
  46.7 23.8 %collective-permute-start.7 = (bf16[2,128,1024]{2,1,0:T(8,128)(2,1)S(1)}, bf16[2,128,1024]{2,1,0:T(8,128)(2,1)}, u32[]{:S(2)}, u32[]{:S(2)}) collective-permute-start(bf16[2,128,1024]{2,1,0:T(8,128)(2,1)S(1)} %collective-permute-done.2.refs_2_.refs_4_.refs_5_), channel_id=1, source_target_pairs={{2,0},{3,1},{4,2},{5,3},{6,4},{7,5},{8,6},{9,7},{10,8},{11,9},{12,... | collective-permute-start | bytes 1572872 | tf_op jit(solution)/shard_map/ppermute | solution.py:289
  50.0 20.5 %copy-start.1 = (bf16[2,128,1024]{2,1,0:T(8,128)(2,1)S(1)}, bf16[2,128,1024]{2,1,0:T(8,128)(2,1)}, u32[]{:S(2)}) copy-start(bf16[2,128,1024]{2,1,0:T(8,128)(2,1)} %copy-done) | copy-start | bytes 1572868
  50.8 1.0 copy-start.3
  51.8 1.0 copy-start.5
  52.9 1.0 copy-start.7
  71.8 12.9 %collective-permute-start.10 = (bf16[12,128,1024]{2,1,0:T(8,128)(2,1)S(1)}, bf16[12,128,1024]{2,1,0:T(8,128)(2,1)S(1)}, u32[]{:S(2)}, u32[]{:S(2)}) collective-permute-start(bf16[12,128,1024]{2,1,0:T(8,128)(2,1)S(1)} %pair_far.1), channel_id=1, source_target_pairs={{0,1},{1,0},{2,3},{3,2},{4,5},{5,4},{6,7},{7,6},{8,9},{9,8},{10,11... | collective-permute-start | bytes 9437192 | tf_op jit(solution)/shard_map/ppermute | solution.py:294

commit v2 on v1

--- a/solution.py
+++ b/solution.py
@@ -306,9 +306,10 @@
     tie = lax.optimization_barrier
     parity = (lax.axis_index("chan") % 2).astype(jnp.int32)[None]
 
-    own_p, own_m, own_2 = (moved(own, "day", by) for by in (1, -1, 2))
-    z2, z4 = moved(own, "chan", -2), moved(own, "chan", -4)
-    own_p, own_m, own_2, z2, z4 = tie((own_p, own_m, own_2, z2, z4))
+    own_2, z2 = moved(own, "day", 2), moved(own, "chan", -2)
+    own_m, own_p = moved(own, "day", -1), moved(own, "day", 1)
+    z4 = moved(own, "chan", -4)
+    own_2, z2, own_m, own_p, z4 = tie((own_2, z2, own_m, own_p, z4))
 
     z2_2, z4_2 = moved(own_2, "chan", -2), moved(own_2, "chan", -4)
     both = [(1, 0, 0, 0, 2), (2, 0, 0, 2, 2)]

time: 106 us -> 104 us (0.981)
  the two profiles are of different devices: /device:TPU:23 before, /device:TPU:14 now
where the time goes in v2:
time: 104 us; the launch traced here: 103 us
  Pallas kernels  48.9 us (47%)
  waiting for transfers between devices  27.9 us (27%)
  starting transfers between devices  20.6 us (20%)
  local copies, waits for them, and re-layouts  4.55 us (4%)
    pallas_call x3, Pallas kernels, correlate(): pl.pallas_call(functools.partial(correlate_kernel, places, arrays, part,...  43.8 us
    ppermute x9, waiting for transfers between devices, moved(): return lax.ppermute(array, axis, pairs)  27.9 us
    ppermute x9, starting transfers between devices, moved(): return lax.ppermute(array, axis, pairs)  20.4 us
    unnamed x16, local copies, waits for them, and re-layouts  4.55 us
    pallas_call x2, Pallas kernels, gather(): pl.pallas_call(functools.partial(gather_kernel, (len(arrays), even, odd))...  2.9 us
    pallas_call x1, Pallas kernels, whiten(): pl.pallas_call(whiten_kernel, in_specs=[pl.BlockSpec(memory_space=pltpu.V...  2.17 us
  transfers between devices with their start and end apart: 11, of which 4 were waited for; matrix products, arithmetic and copies ran while one was open for 1% of the time, Pallas kernels for 23%

profile of v2, /device:TPU:14, one launch (start us, length us, event | category | flops | bytes accessed | tf_op | source)
XLA Modules:
  0.0 103.0 jit_solution(9401364553473871071)
XLA Ops:
  0.0 2.2 %whiten.1.refs_0_ = bf16[2,128,1024]{2,1,0:T(8,128)(2,1)} custom-call(bf16[2,128,1024]{2,1,0:T(8,128)(2,1)} %raw_ref.1), custom_call_target="tpu_custom_call" | custom-call | flops 2097152 | bytes 1048576 | tf_op jit(solution)/shard_map/whiten/pallas_call | solution.py:29
  2.2 5.7 %collective-permute-start.4 = (bf16[2,128,1024]{2,1,0:T(8,128)(2,1)}, bf16[2,128,1024]{2,1,0:T(8,128)(2,1)S(1)}, u32[]{:S(2)}, u32[]{:S(2)}) collective-permute-start(bf16[2,128,1024]{2,1,0:T(8,128)(2,1)} %whiten.1.refs_0_), channel_id=1, source_target_pairs={{4,0},{5,1},{6,2},{7,3},{8,4},{9,5},{10,6},{11,7},{12,8},{13,9},{1... | collective-permute-start | bytes 1572872 | tf_op jit(solution)/shard_map/ppermute | solution.py:289
  7.8 0.5 collective-permute-start.3
  8.4 1.5 %collective-permute-start.2 = (bf16[2,128,1024]{2,1,0:T(8,128)(2,1)}, bf16[2,128,1024]{2,1,0:T(8,128)(2,1)S(1)}, u32[]{:S(2)}, u32[]{:S(2)}) collective-permute-start(bf16[2,128,1024]{2,1,0:T(8,128)(2,1)} %whiten.1.refs_0_), channel_id=1, source_target_pairs={{0,96},{32,0},{64,32},{96,64},{1,97},{33,1},{65,33},{97,65},{2,98}... | collective-permute-start | bytes 1572872 | tf_op jit(solution)/shard_map/ppermute | solution.py:289
  9.9 2.6 %collective-permute-start.1 = (bf16[2,128,1024]{2,1,0:T(8,128)(2,1)}, bf16[2,128,1024]{2,1,0:T(8,128)(2,1)S(1)}, u32[]{:S(2)}, u32[]{:S(2)}) collective-permute-start(bf16[2,128,1024]{2,1,0:T(8,128)(2,1)} %whiten.1.refs_0_), channel_id=1, source_target_pairs={{2,0},{3,1},{4,2},{5,3},{6,4},{7,5},{8,6},{9,7},{10,8},{11,9},{12,... | collective-permute-start | bytes 1572872 | tf_op jit(solution)/shard_map/ppermute | solution.py:289
  12.5 1.5 %collective-permute-start = (bf16[2,128,1024]{2,1,0:T(8,128)(2,1)}, bf16[2,128,1024]{2,1,0:T(8,128)(2,1)S(1)}, u32[]{:S(2)}, u32[]{:S(2)}) collective-permute-start(bf16[2,128,1024]{2,1,0:T(8,128)(2,1)} %whiten.1.refs_0_), channel_id=1, source_target_pairs={{0,64},{32,96},{64,0},{96,32},{1,65},{33,97},{65,1},{97,33},{2,66}... | collective-permute-start | bytes 1572872 | tf_op jit(solution)/shard_map/ppermute | solution.py:289
  14.0 6.4 %collective-permute-done.4.refs_2_.refs_3_ = bf16[2,128,1024]{2,1,0:T(8,128)(2,1)S(1)} collective-permute-done((bf16[2,128,1024]{2,1,0:T(8,128)(2,1)}, bf16[2,128,1024]{2,1,0:T(8,128)(2,1)S(1)}, u32[]{:S(2)}, u32[]{:S(2)}) %collective-permute-start.4) | collective-permute-done | bytes 524320 | tf_op jit(solution)/shard_map/ppermute | solution.py:289
  20.5 0.0 copy-start.4
  20.5 2.5 %collective-permute-done.3.refs_0_ = bf16[2,128,1024]{2,1,0:T(8,128)(2,1)S(1)} collective-permute-done((bf16[2,128,1024]{2,1,0:T(8,128)(2,1)}, bf16[2,128,1024]{2,1,0:T(8,128)(2,1)S(1)}, u32[]{:S(2)}, u32[]{:S(2)}) %collective-permute-start.3) | collective-permute-done | bytes 524320 | tf_op jit(solution)/shard_map/ppermute | solution.py:289
  23.0 11.2 %collective-permute-done.2.refs_1_.refs_2_.refs_3_ = bf16[2,128,1024]{2,1,0:T(8,128)(2,1)S(1)} collective-permute-done((bf16[2,128,1024]{2,1,0:T(8,128)(2,1)}, bf16[2,128,1024]{2,1,0:T(8,128)(2,1)S(1)}, u32[]{:S(2)}, u32[]{:S(2)}) %collective-permute-start.2) | collective-permute-done | bytes 524320 | tf_op jit(solution)/shard_map/ppermute | solution.py:289
  34.1 0.0 collective-permute-done.1.refs_1_.refs_2_
  34.1 0.0 copy-start.6
  34.1 0.0 collective-permute-done.refs_2_.refs_4_.refs_5_
  34.2 0.0 copy-start
  34.2 0.0 copy-start.2
  34.2 1.4 %copy-done.2 = bf16[2,128,1024]{2,1,0:T(8,128)(2,1)S(1)} copy-done((bf16[2,128,1024]{2,1,0:T(8,128)(2,1)S(1)}, bf16[2,128,1024]{2,1,0:T(8,128)(2,1)}, u32[]{:S(2)}) %copy-start.2) | copy-done | bytes 524312
  35.6 1.5 %pair_near.1 = (bf16[4,128,1024]{2,1,0:T(8,128)(2,1)}, bf16[4,128,1024]{2,1,0:T(8,128)(2,1)}) custom-call(s32[1]{0:T(128)} %bitcast.2.flag, bf16[2,128,1024]{2,1,0:T(8,128)(2,1)S(1)} %copy-done.2, bf16[2,128,1024]{2,1,0:T(8,128)(2,1)S(1)} %collective-permute-done.1.refs_1_.refs_2_, bf16[2,128,1024]{2,1,0:T(8,128)(2,1)S(1)} %collective-permute-done.4.refs_2_.refs_3_), custom_call_target="tpu_custom_call" | custom-call | tf_op jit(solution)/shard_map/pair_near/pallas_call | solution.py:63
  37.1 0.1 collective-permute-start.9
  37.2 0.0 copy-done.4
  37.2 0.0 copy-done
  37.2 0.0 copy-done.6
  37.2 0.1 collective-permute-start.6
  37.3 3.2 %collective-permute-start.5 = (bf16[4,128,1024]{2,1,0:T(8,128)(2,1)}, bf16[4,128,1024]{2,1,0:T(8,128)(2,1)S(1)}, u32[]{:S(2)}, u32[]{:S(2)}) collective-permute-start(bf16[4,128,1024]{2,1,0:T(8,128)(2,1)} %get-tuple-element.22), channel_id=1, source_target_pairs={{0,32},{32,64},{64,96},{96,0},{1,33},{33,65},{65,97},{97,1},{2,34}... | collective-permute-start | bytes 3145736 | tf_op jit(solution)/shard_map/ppermute | solution.py:289
  40.5 2.2 %collective-permute-start.8 = (bf16[2,128,1024]{2,1,0:T(8,128)(2,1)}, bf16[2,128,1024]{2,1,0:T(8,128)(2,1)}, u32[]{:S(2)}, u32[]{:S(2)}) collective-permute-start(bf16[2,128,1024]{2,1,0:T(8,128)(2,1)} %copy-done), channel_id=1, source_target_pairs={{4,0},{5,1},{6,2},{7,3},{8,4},{9,5},{10,6},{11,7},{12,8},{13,9},{1... | collective-permute-start | bytes 1572872 | tf_op jit(solution)/shard_map/ppermute | solution.py:289
  42.7 3.1 %collective-permute-start.7 = (bf16[2,128,1024]{2,1,0:T(8,128)(2,1)}, bf16[2,128,1024]{2,1,0:T(8,128)(2,1)}, u32[]{:S(2)}, u32[]{:S(2)}) collective-permute-start(bf16[2,128,1024]{2,1,0:T(8,128)(2,1)} %copy-done), channel_id=1, source_target_pairs={{2,0},{3,1},{4,2},{5,3},{6,4},{7,5},{8,6},{9,7},{10,8},{11,9},{12,... | collective-permute-start | bytes 1572872 | tf_op jit(solution)/shard_map/ppermute | solution.py:289
  45.8 0.0 copy-start.1
  45.8 0.8 pad_add_fusion.win
  46.6 0.0 collective-permute-done.9.refs_1_
  46.6 0.0 copy-start.3
  46.6 1.0 %copy-done.3 = bf16[2,128,1024]{2,1,0:T(8,128)(2,1)S(1)} copy-done((bf16[2,128,1024]{2,1,0:T(8,128)(2,1)S(1)}, bf16[2,128,1024]{2,1,0:T(8,128)(2,1)}, u32[]{:S(2)}) %copy-start.3) | copy-done | bytes 524312
  47.6 0.0 copy-start.5
  47.6 1.0 %copy-done.5 = bf16[2,128,1024]{2,1,0:T(8,128)(2,1)S(1)} copy-done((bf16[2,128,1024]{2,1,0:T(8,128)(2,1)S(1)}, bf16[2,128,1024]{2,1,0:T(8,128)(2,1)}, u32[]{:S(2)}) %copy-start.5) | copy-done | bytes 524312
  48.7 0.0 copy-start.7
  48.7 1.0 %copy-done.7 = bf16[2,128,1024]{2,1,0:T(8,128)(2,1)S(1)} copy-done((bf16[2,128,1024]{2,1,0:T(8,128)(2,1)S(1)}, bf16[2,128,1024]{2,1,0:T(8,128)(2,1)}, u32[]{:S(2)}) %copy-start.7) | copy-done | bytes 524312
  49.7 11.5 %near_days.1.refs_7_ = f32[3,129,32,128]{3,2,1,0:T(8,128)} custom-call(s32[4]{0:T(128)S(1)} %pad_add_fusion.win, bf16[2,128,1024]{2,1,0:T(8,128)(2,1)S(1)} %copy-done.3, bf16[4,128,1024]{2,1,0:T(8,128)(2,1)} %collective-permute-done.9.refs_1_, bf16[2,128,1024]{2,1,0:T(8,128)(2,1)S(1)} %copy-done.7, bf16[2,128,1024]{2,1,0:T(8,128)(2,1)S(1)} %copy-done.5), custom_call_target="tpu_custom_call" | custom-call | flops 1048576 | bytes 65536 | tf_op jit(solution)/shard_map/near_days/pallas_call | solution.py:249
  61.2 0.0 collective-permute-done.8.refs_6_.refs_7_
  61.2 7.7 %collective-permute-done.7.refs_5_.refs_6_ = bf16[2,128,1024]{2,1,0:T(8,128)(2,1)} collective-permute-done((bf16[2,128,1024]{2,1,0:T(8,128)(2,1)}, bf16[2,128,1024]{2,1,0:T(8,128)(2,1)}, u32[]{:S(2)}, u32[]{:S(2)}) %collective-permute-start.7) | collective-permute-done | bytes 524320 | tf_op jit(solution)/shard_map/ppermute | solution.py:289
  69.0 0.0 collective-permute-done.6.refs_4_.refs_3_
  69.0 0.0 collective-permute-done.5.refs_3_.refs_1_.refs_2_
  69.0 0.0 copy-done.1
  69.0 1.4 %pair_far.1 = bf16[12,128,1024]{2,1,0:T(8,128)(2,1)S(1)} custom-call(s32[1]{0:T(128)} %bitcast.2.flag, bf16[2,128,1024]{2,1,0:T(8,128)(2,1)S(1)} %collective-permute-done.3.refs_0_, bf16[2,128,1024]{2,1,0:T(8,128)(2,1)S(1)} %collective-permute-done.2.refs_1_.refs_2_.refs_3_, bf16[2,128,1024]{2,1,0:T(8,128)(2,1)S(1)} %copy-done.1, ...), custom_call_target="tpu_custom_call" | custom-call | tf_op jit(solution)/shard_map/pair_far/pallas_call | solution.py:63
  70.4 0.1 collective-permute-start.10
  70.5 12.2 %far_days_one.1.refs_8_ = f32[3,129,32,128]{3,2,1,0:T(8,128)} custom-call(s32[4]{0:T(128)S(1)} %pad_add_fusion.win, bf16[2,128,1024]{2,1,0:T(8,128)(2,1)S(1)} %collective-permute-done.3.refs_0_, bf16[4,128,1024]{2,1,0:T(8,128)(2,1)S(1)} %collective-permute-done.5.refs_3_.refs_1_.refs_2_, ...), custom_call_target="tpu_custom_call", output_to_operand_aliasing={{}: (8, {})} | custom-call | flops 1048576 | bytes 65536 | tf_op jit(solution)/shard_map/far_days_one/pallas_call | solution.py:249
  82.7 0.0 collective-permute-done.10.refs_1_
  82.7 20.1 %far_days_rest.1 = f32[3,129,32,128]{3,2,1,0:T(8,128)} custom-call(s32[4]{0:T(128)S(1)} %pad_add_fusion.win, bf16[2,128,1024]{2,1,0:T(8,128)(2,1)S(1)} %collective-permute-done.3.refs_0_, bf16[12,128,1024]{2,1,0:T(8,128)(2,1)S(1)} %collective-permute-done.10.refs_1_, ...), custom_call_target="tpu_custom_call", output_to_operand_aliasing={{}: (9, {})} | custom-call | flops 1048576 | bytes 65536 | tf_op jit(solution)/shard_map/far_days_rest/pallas_call | solution.py:249
Async XLA Ops:
  2.2 18.3 %collective-permute-start.4 = (bf16[2,128,1024]{2,1,0:T(8,128)(2,1)}, bf16[2,128,1024]{2,1,0:T(8,128)(2,1)S(1)}, u32[]{:S(2)}, u32[]{:S(2)}) collective-permute-start(bf16[2,128,1024]{2,1,0:T(8,128)(2,1)} %whiten.1.refs_0_), channel_id=1, source_target_pairs={{4,0},{5,1},{6,2},{7,3},{8,4},{9,5},{10,6},{11,7},{12,8},{13,9},{1... | collective-permute-start | bytes 1572872 | tf_op jit(solution)/shard_map/ppermute | solution.py:289
  7.8 15.1 %collective-permute-start.3 = (bf16[2,128,1024]{2,1,0:T(8,128)(2,1)}, bf16[2,128,1024]{2,1,0:T(8,128)(2,1)S(1)}, u32[]{:S(2)}, u32[]{:S(2)}) collective-permute-start(bf16[2,128,1024]{2,1,0:T(8,128)(2,1)} %whiten.1.refs_0_), channel_id=1, source_target_pairs={{0,32},{32,64},{64,96},{96,0},{1,33},{33,65},{65,97},{97,1},{2,34}... | collective-permute-start | bytes 1572872 | tf_op jit(solution)/shard_map/ppermute | solution.py:289
  8.4 25.8 %collective-permute-start.2 = (bf16[2,128,1024]{2,1,0:T(8,128)(2,1)}, bf16[2,128,1024]{2,1,0:T(8,128)(2,1)S(1)}, u32[]{:S(2)}, u32[]{:S(2)}) collective-permute-start(bf16[2,128,1024]{2,1,0:T(8,128)(2,1)} %whiten.1.refs_0_), channel_id=1, source_target_pairs={{0,96},{32,0},{64,32},{96,64},{1,97},{33,1},{65,33},{97,65},{2,98}... | collective-permute-start | bytes 1572872 | tf_op jit(solution)/shard_map/ppermute | solution.py:289
  9.9 24.2 %collective-permute-start.1 = (bf16[2,128,1024]{2,1,0:T(8,128)(2,1)}, bf16[2,128,1024]{2,1,0:T(8,128)(2,1)S(1)}, u32[]{:S(2)}, u32[]{:S(2)}) collective-permute-start(bf16[2,128,1024]{2,1,0:T(8,128)(2,1)} %whiten.1.refs_0_), channel_id=1, source_target_pairs={{2,0},{3,1},{4,2},{5,3},{6,4},{7,5},{8,6},{9,7},{10,8},{11,9},{12,... | collective-permute-start | bytes 1572872 | tf_op jit(solution)/shard_map/ppermute | solution.py:289
  12.5 21.6 %collective-permute-start = (bf16[2,128,1024]{2,1,0:T(8,128)(2,1)}, bf16[2,128,1024]{2,1,0:T(8,128)(2,1)S(1)}, u32[]{:S(2)}, u32[]{:S(2)}) collective-permute-start(bf16[2,128,1024]{2,1,0:T(8,128)(2,1)} %whiten.1.refs_0_), channel_id=1, source_target_pairs={{0,64},{32,96},{64,0},{96,32},{1,65},{33,97},{65,1},{97,33},{2,66}... | collective-permute-start | bytes 1572872 | tf_op jit(solution)/shard_map/ppermute | solution.py:289
  20.5 16.7 %copy-start.4 = (bf16[2,128,1024]{2,1,0:T(8,128)(2,1)}, bf16[2,128,1024]{2,1,0:T(8,128)(2,1)S(1)}, u32[]{:S(2)}) copy-start(bf16[2,128,1024]{2,1,0:T(8,128)(2,1)S(1)} %collective-permute-done.4.refs_2_.refs_3_) | copy-start | bytes 1572868
  34.1 3.1 %copy-start.6 = (bf16[2,128,1024]{2,1,0:T(8,128)(2,1)}, bf16[2,128,1024]{2,1,0:T(8,128)(2,1)S(1)}, u32[]{:S(2)}) copy-start(bf16[2,128,1024]{2,1,0:T(8,128)(2,1)S(1)} %collective-permute-done.1.refs_1_.refs_2_) | copy-start | bytes 1572868
  34.2 3.0 %copy-start = (bf16[2,128,1024]{2,1,0:T(8,128)(2,1)}, bf16[2,128,1024]{2,1,0:T(8,128)(2,1)S(1)}, u32[]{:S(2)}) copy-start(bf16[2,128,1024]{2,1,0:T(8,128)(2,1)S(1)} %collective-permute-done.refs_2_.refs_4_.refs_5_) | copy-start | bytes 1572868
  34.2 1.4 %copy-start.2 = (bf16[2,128,1024]{2,1,0:T(8,128)(2,1)S(1)}, bf16[2,128,1024]{2,1,0:T(8,128)(2,1)}, u32[]{:S(2)}) copy-start(bf16[2,128,1024]{2,1,0:T(8,128)(2,1)} %whiten.1.refs_0_) | copy-start | bytes 1572868
  37.1 9.5 %collective-permute-start.9 = (bf16[4,128,1024]{2,1,0:T(8,128)(2,1)}, bf16[4,128,1024]{2,1,0:T(8,128)(2,1)}, u32[]{:S(2)}, u32[]{:S(2)}) collective-permute-start(bf16[4,128,1024]{2,1,0:T(8,128)(2,1)} %get-tuple-element.23), channel_id=1, source_target_pairs={{0,1},{1,0},{2,3},{3,2},{4,5},{5,4},{6,7},{7,6},{8,9},{9,8},{10,11... | collective-permute-start | bytes 3145736 | tf_op jit(solution)/shard_map/ppermute | solution.py:294
  37.2 31.8 %collective-permute-start.6 = (bf16[4,128,1024]{2,1,0:T(8,128)(2,1)}, bf16[4,128,1024]{2,1,0:T(8,128)(2,1)S(1)}, u32[]{:S(2)}, u32[]{:S(2)}) collective-permute-start(bf16[4,128,1024]{2,1,0:T(8,128)(2,1)} %get-tuple-element.22), channel_id=1, source_target_pairs={{0,96},{32,0},{64,32},{96,64},{1,97},{33,1},{65,33},{97,65},{2,98}... | collective-permute-start | bytes 3145736 | tf_op jit(solution)/shard_map/ppermute | solution.py:289
  37.3 31.7 %collective-permute-start.5 = (bf16[4,128,1024]{2,1,0:T(8,128)(2,1)}, bf16[4,128,1024]{2,1,0:T(8,128)(2,1)S(1)}, u32[]{:S(2)}, u32[]{:S(2)}) collective-permute-start(bf16[4,128,1024]{2,1,0:T(8,128)(2,1)} %get-tuple-element.22), channel_id=1, source_target_pairs={{0,32},{32,64},{64,96},{96,0},{1,33},{33,65},{65,97},{97,1},{2,34}... | collective-permute-start | bytes 3145736 | tf_op jit(solution)/shard_map/ppermute | solution.py:289
  40.5 20.7 %collective-permute-start.8 = (bf16[2,128,1024]{2,1,0:T(8,128)(2,1)}, bf16[2,128,1024]{2,1,0:T(8,128)(2,1)}, u32[]{:S(2)}, u32[]{:S(2)}) collective-permute-start(bf16[2,128,1024]{2,1,0:T(8,128)(2,1)} %copy-done), channel_id=1, source_target_pairs={{4,0},{5,1},{6,2},{7,3},{8,4},{9,5},{10,6},{11,7},{12,8},{13,9},{1... | collective-permute-start | bytes 1572872 | tf_op jit(solution)/shard_map/ppermute | solution.py:289
  42.7 26.2 %collective-permute-start.7 = (bf16[2,128,1024]{2,1,0:T(8,128)(2,1)}, bf16[2,128,1024]{2,1,0:T(8,128)(2,1)}, u32[]{:S(2)}, u32[]{:S(2)}) collective-permute-start(bf16[2,128,1024]{2,1,0:T(8,128)(2,1)} %copy-done), channel_id=1, source_target_pairs={{2,0},{3,1},{4,2},{5,3},{6,4},{7,5},{8,6},{9,7},{10,8},{11,9},{12,... | collective-permute-start | bytes 1572872 | tf_op jit(solution)/shard_map/ppermute | solution.py:289
  45.8 23.2 %copy-start.1 = (bf16[2,128,1024]{2,1,0:T(8,128)(2,1)S(1)}, bf16[2,128,1024]{2,1,0:T(8,128)(2,1)}, u32[]{:S(2)}) copy-start(bf16[2,128,1024]{2,1,0:T(8,128)(2,1)} %copy-done) | copy-start | bytes 1572868
  46.6 1.0 %copy-start.3 = (bf16[2,128,1024]{2,1,0:T(8,128)(2,1)S(1)}, bf16[2,128,1024]{2,1,0:T(8,128)(2,1)}, u32[]{:S(2)}) copy-start(bf16[2,128,1024]{2,1,0:T(8,128)(2,1)} %whiten.1.refs_0_) | copy-start | bytes 1572868
  47.6 1.0 %copy-start.5 = (bf16[2,128,1024]{2,1,0:T(8,128)(2,1)S(1)}, bf16[2,128,1024]{2,1,0:T(8,128)(2,1)}, u32[]{:S(2)}) copy-start(bf16[2,128,1024]{2,1,0:T(8,128)(2,1)} %copy-done.4) | copy-start | bytes 1572868
  48.7 1.0 %copy-start.7 = (bf16[2,128,1024]{2,1,0:T(8,128)(2,1)S(1)}, bf16[2,128,1024]{2,1,0:T(8,128)(2,1)}, u32[]{:S(2)}) copy-start(bf16[2,128,1024]{2,1,0:T(8,128)(2,1)} %copy-done.6) | copy-start | bytes 1572868
  70.4 12.3 %collective-permute-start.10 = (bf16[12,128,1024]{2,1,0:T(8,128)(2,1)S(1)}, bf16[12,128,1024]{2,1,0:T(8,128)(2,1)S(1)}, u32[]{:S(2)}, u32[]{:S(2)}) collective-permute-start(bf16[12,128,1024]{2,1,0:T(8,128)(2,1)S(1)} %pair_far.1), channel_id=1, source_target_pairs={{0,1},{1,0},{2,3},{3,2},{4,5},{5,4},{6,7},{7,6},{8,9},{9,8},{10,11... | collective-permute-start | bytes 9437192 | tf_op jit(solution)/shard_map/ppermute | solution.py:294

commit v3 on v2

--- a/solution.py
+++ b/solution.py
@@ -107,6 +107,12 @@
     def copy_out(k, seat):
         return pltpu.make_async_copy(tiles.at[seat], out_ref.at[k], sem_out.at[seat])
 
+    def copy_lags(k, seat, at, to):
+        lags = pl.ds(at, to - at)
+        return pltpu.make_async_copy(
+            tiles.at[seat, lags], out_ref.at[k, lags], sem_out.at[seat]
+        )
+
     def copy_zero(k):
         return pltpu.make_async_copy(before, out_ref.at[k], sem_in.at[k])
 
@@ -126,15 +132,15 @@
     def _():
         for s in range(sets):
             copy_left(s).start()
-        for k in range(TILES_DEV):
-            for e in range(0, REACH + 1, 2 if part == "head" else 1):
-
-                @pl.when(jnp.logical_and(lives[k], win[1 + k] == e))
-                def _():
-                    for s in range(sets):
+            for k in range(TILES_DEV):
+                for e in range(0, REACH + 1, 2 if part == "head" else 1):
+
+                    @pl.when(jnp.logical_and(lives[k], win[1 + k] == e))
+                    def _():
                         copy_right(s, seats[k], e).start()
 
-            if not first:
+        if not first:
+            for k in range(TILES_DEV):
 
                 @pl.when(lives[k])
                 def _():
@@ -169,16 +175,24 @@
                 [p for d in range(days) for p in (braw[seat, s, d], gap_b)], 1
             )
 
-        def work(seat, with_shift):
-            for s in range(sets):
+        def work(k, seat, with_shift):
+            late = part == "head"
+            for s in range(1 if late else sets):
                 copy_right(s, seat, 0).wait()
-                make_right(s, seat)
-            if not first:
+            if not first and not late:
                 copy_in(0, seat).wait()
+            make_right(0, seat)
             if with_shift:
                 make_shift(0, 0)
             for n in range(sets * GROUPS):
                 s, g = divmod(n, GROUPS)
+                if late and n == 1:
+                    for r in range(1, sets):
+                        copy_right(r, seat, 0).wait()
+                if g == 1 and s + 1 < sets:
+                    make_right(s + 1, seat)
+                if late and n == (sets - 1) * GROUPS:
+                    copy_in(0, seat).wait()
                 if with_shift and n + 1 < sets * GROUPS:
                     make_shift(*divmod(n + 1, GROUPS))
                 product = lax.dot_general(
@@ -203,14 +217,18 @@
                         tiles[seat, at] = value * norm
                     else:
                         tiles[seat, at] = value * norm + before[seat, at]
+                if s + 1 == sets and g >= GROUPS - 2:
+                    at, to = (0, g * GROUP + GROUP) if g < GROUPS - 1 else (g * GROUP, MAXLAG)
+                    copy_lags(k, seat, at, to).start()
+                    copy_lags(k, seat, MAXLAG + at, LAGS if to == MAXLAG else MAXLAG + to).start()
 
         def loop(seat, carry):
-            pl.when(seat == 0)(functools.partial(work, seat, True))
+            k = jnp.int32(0)
+            for n in range(TILES_DEV):
+                k = jnp.where(jnp.logical_and(lives[n], seats[n] == seat), n, k)
+            pl.when(seat == 0)(functools.partial(work, k, seat, True))
             if slots > 1:
-                pl.when(seat > 0)(functools.partial(work, seat, False))
-            for k in range(TILES_DEV):
-                mine = jnp.logical_and(lives[k], seats[k] == seat)
-                pl.when(mine)(copy_out(k, seat).start)
+                pl.when(seat > 0)(functools.partial(work, k, seat, False))
             return carry
 
         lax.fori_loop(0, seats[-1], loop, 0)

time: 104 us -> 103 us (level)
  the two profiles are of different devices: /device:TPU:14 before, /device:TPU:15 now
where the time goes in v3:
time: 103 us
  Pallas kernels  47.8 us (46%)
  waiting for transfers between devices  28.7 us (28%)
  starting transfers between devices  20.6 us (20%)
  local copies, waits for them, and re-layouts  4.56 us (4%)
    pallas_call x3, Pallas kernels, correlate(): pl.pallas_call(functools.partial(correlate_kernel, places, arrays, part,...  42.8 us
    ppermute x9, waiting for transfers between devices, moved(): return lax.ppermute(array, axis, pairs)  28.7 us
    ppermute x9, starting transfers between devices, moved(): return lax.ppermute(array, axis, pairs)  18.2 us
    unnamed x16, local copies, waits for them, and re-layouts  4.56 us
    pallas_call x2, Pallas kernels, gather(): pl.pallas_call(functools.partial(gather_kernel, (len(arrays), even, odd))...  2.79 us
    ppermute x2, starting transfers between devices, swapped(): return lax.ppermute(array, 'chan', [(i, i ^ 1) for i in range(devices)])  2.49 us
    pallas_call x1, Pallas kernels, whiten(): pl.pallas_call(whiten_kernel, in_specs=[pl.BlockSpec(memory_space=pltpu.V...  2.17 us
  transfers between devices with their start and end apart: 11, of which 5 were waited for; matrix products, arithmetic and copies ran while one was open for 1% of the time, Pallas kernels for 22%

profile of v3, /device:TPU:15, one launch (start us, length us, event | category | flops | bytes accessed | tf_op | source)
XLA Modules:
  0.0 102.8 jit_solution(11691898560803086061)
XLA Ops:
  0.0 2.2 %whiten.1.refs_0_ = bf16[2,128,1024]{2,1,0:T(8,128)(2,1)} custom-call(bf16[2,128,1024]{2,1,0:T(8,128)(2,1)} %raw_ref.1), custom_call_target="tpu_custom_call" | custom-call | flops 2097152 | bytes 1048576 | tf_op jit(solution)/shard_map/whiten/pallas_call | solution.py:29
  2.2 5.4 %collective-permute-start.4 = (bf16[2,128,1024]{2,1,0:T(8,128)(2,1)}, bf16[2,128,1024]{2,1,0:T(8,128)(2,1)S(1)}, u32[]{:S(2)}, u32[]{:S(2)}) collective-permute-start(bf16[2,128,1024]{2,1,0:T(8,128)(2,1)} %whiten.1.refs_0_), channel_id=1, source_target_pairs={{4,0},{5,1},{6,2},{7,3},{8,4},{9,5},{10,6},{11,7},{12,8},{13,9},{1... | collective-permute-start | bytes 1572872 | tf_op jit(solution)/shard_map/ppermute | solution.py:307
  7.6 0.3 collective-permute-start.3
  7.8 1.3 %collective-permute-start.2 = (bf16[2,128,1024]{2,1,0:T(8,128)(2,1)}, bf16[2,128,1024]{2,1,0:T(8,128)(2,1)S(1)}, u32[]{:S(2)}, u32[]{:S(2)}) collective-permute-start(bf16[2,128,1024]{2,1,0:T(8,128)(2,1)} %whiten.1.refs_0_), channel_id=1, source_target_pairs={{0,96},{32,0},{64,32},{96,64},{1,97},{33,1},{65,33},{97,65},{2,98}... | collective-permute-start | bytes 1572872 | tf_op jit(solution)/shard_map/ppermute | solution.py:307
  9.1 2.3 %collective-permute-start.1 = (bf16[2,128,1024]{2,1,0:T(8,128)(2,1)}, bf16[2,128,1024]{2,1,0:T(8,128)(2,1)S(1)}, u32[]{:S(2)}, u32[]{:S(2)}) collective-permute-start(bf16[2,128,1024]{2,1,0:T(8,128)(2,1)} %whiten.1.refs_0_), channel_id=1, source_target_pairs={{2,0},{3,1},{4,2},{5,3},{6,4},{7,5},{8,6},{9,7},{10,8},{11,9},{12,... | collective-permute-start | bytes 1572872 | tf_op jit(solution)/shard_map/ppermute | solution.py:307
  11.4 1.2 %collective-permute-start = (bf16[2,128,1024]{2,1,0:T(8,128)(2,1)}, bf16[2,128,1024]{2,1,0:T(8,128)(2,1)S(1)}, u32[]{:S(2)}, u32[]{:S(2)}) collective-permute-start(bf16[2,128,1024]{2,1,0:T(8,128)(2,1)} %whiten.1.refs_0_), channel_id=1, source_target_pairs={{0,64},{32,96},{64,0},{96,32},{1,65},{33,97},{65,1},{97,33},{2,66}... | collective-permute-start | bytes 1572872 | tf_op jit(solution)/shard_map/ppermute | solution.py:307
  12.6 6.9 %collective-permute-done.4.refs_2_.refs_3_ = bf16[2,128,1024]{2,1,0:T(8,128)(2,1)S(1)} collective-permute-done((bf16[2,128,1024]{2,1,0:T(8,128)(2,1)}, bf16[2,128,1024]{2,1,0:T(8,128)(2,1)S(1)}, u32[]{:S(2)}, u32[]{:S(2)}) %collective-permute-start.4) | collective-permute-done | bytes 524320 | tf_op jit(solution)/shard_map/ppermute | solution.py:307
  19.5 0.0 copy-start.4
  19.5 0.8 collective-permute-done.3.refs_0_
  20.3 1.4 %collective-permute-done.2.refs_1_.refs_2_.refs_3_ = bf16[2,128,1024]{2,1,0:T(8,128)(2,1)S(1)} collective-permute-done((bf16[2,128,1024]{2,1,0:T(8,128)(2,1)}, bf16[2,128,1024]{2,1,0:T(8,128)(2,1)S(1)}, u32[]{:S(2)}, u32[]{:S(2)}) %collective-permute-start.2) | collective-permute-done | bytes 524320 | tf_op jit(solution)/shard_map/ppermute | solution.py:307
  21.7 11.4 %collective-permute-done.1.refs_1_.refs_2_ = bf16[2,128,1024]{2,1,0:T(8,128)(2,1)S(1)} collective-permute-done((bf16[2,128,1024]{2,1,0:T(8,128)(2,1)}, bf16[2,128,1024]{2,1,0:T(8,128)(2,1)S(1)}, u32[]{:S(2)}, u32[]{:S(2)}) %collective-permute-start.1) | collective-permute-done | bytes 524320 | tf_op jit(solution)/shard_map/ppermute | solution.py:307
  33.1 0.0 copy-start.6
  33.1 0.0 collective-permute-done.refs_2_.refs_4_.refs_5_
  33.1 0.0 copy-start
  33.1 0.0 copy-start.2
  33.1 1.4 %copy-done.2 = bf16[2,128,1024]{2,1,0:T(8,128)(2,1)S(1)} copy-done((bf16[2,128,1024]{2,1,0:T(8,128)(2,1)S(1)}, bf16[2,128,1024]{2,1,0:T(8,128)(2,1)}, u32[]{:S(2)}) %copy-start.2) | copy-done | bytes 524312
  34.5 1.5 %pair_near.1 = (bf16[4,128,1024]{2,1,0:T(8,128)(2,1)}, bf16[4,128,1024]{2,1,0:T(8,128)(2,1)}) custom-call(s32[1]{0:T(128)} %bitcast.2.flag, bf16[2,128,1024]{2,1,0:T(8,128)(2,1)S(1)} %copy-done.2, bf16[2,128,1024]{2,1,0:T(8,128)(2,1)S(1)} %collective-permute-done.1.refs_1_.refs_2_, bf16[2,128,1024]{2,1,0:T(8,128)(2,1)S(1)} %collective-permute-done.4.refs_2_.refs_3_), custom_call_target="tpu_custom_call" | custom-call | tf_op jit(solution)/shard_map/pair_near/pallas_call | solution.py:63
  36.0 1.8 %collective-permute-start.9 = (bf16[4,128,1024]{2,1,0:T(8,128)(2,1)}, bf16[4,128,1024]{2,1,0:T(8,128)(2,1)}, u32[]{:S(2)}, u32[]{:S(2)}) collective-permute-start(bf16[4,128,1024]{2,1,0:T(8,128)(2,1)} %get-tuple-element.23), channel_id=1, source_target_pairs={{0,1},{1,0},{2,3},{3,2},{4,5},{5,4},{6,7},{7,6},{8,9},{9,8},{10,11... | collective-permute-start | bytes 3145736 | tf_op jit(solution)/shard_map/ppermute | solution.py:312
  37.9 0.0 copy-done.4
  37.9 0.0 copy-done
  37.9 0.0 copy-done.6
  37.9 0.1 collective-permute-start.6
  37.9 2.7 %collective-permute-start.5 = (bf16[4,128,1024]{2,1,0:T(8,128)(2,1)}, bf16[4,128,1024]{2,1,0:T(8,128)(2,1)S(1)}, u32[]{:S(2)}, u32[]{:S(2)}) collective-permute-start(bf16[4,128,1024]{2,1,0:T(8,128)(2,1)} %get-tuple-element.22), channel_id=1, source_target_pairs={{0,32},{32,64},{64,96},{96,0},{1,33},{33,65},{65,97},{97,1},{2,34}... | collective-permute-start | bytes 3145736 | tf_op jit(solution)/shard_map/ppermute | solution.py:307
  40.6 1.9 %collective-permute-start.8 = (bf16[2,128,1024]{2,1,0:T(8,128)(2,1)}, bf16[2,128,1024]{2,1,0:T(8,128)(2,1)}, u32[]{:S(2)}, u32[]{:S(2)}) collective-permute-start(bf16[2,128,1024]{2,1,0:T(8,128)(2,1)} %copy-done), channel_id=1, source_target_pairs={{4,0},{5,1},{6,2},{7,3},{8,4},{9,5},{10,6},{11,7},{12,8},{13,9},{1... | collective-permute-start | bytes 1572872 | tf_op jit(solution)/shard_map/ppermute | solution.py:307
  42.5 3.1 %collective-permute-start.7 = (bf16[2,128,1024]{2,1,0:T(8,128)(2,1)}, bf16[2,128,1024]{2,1,0:T(8,128)(2,1)}, u32[]{:S(2)}, u32[]{:S(2)}) collective-permute-start(bf16[2,128,1024]{2,1,0:T(8,128)(2,1)} %copy-done), channel_id=1, source_target_pairs={{2,0},{3,1},{4,2},{5,3},{6,4},{7,5},{8,6},{9,7},{10,8},{11,9},{12,... | collective-permute-start | bytes 1572872 | tf_op jit(solution)/shard_map/ppermute | solution.py:307
  45.6 0.0 copy-start.1
  45.6 0.8 pad_add_fusion.win
  46.4 0.0 collective-permute-done.9.refs_1_
  46.4 0.0 copy-start.3
  46.4 1.0 %copy-done.3 = bf16[2,128,1024]{2,1,0:T(8,128)(2,1)S(1)} copy-done((bf16[2,128,1024]{2,1,0:T(8,128)(2,1)S(1)}, bf16[2,128,1024]{2,1,0:T(8,128)(2,1)}, u32[]{:S(2)}) %copy-start.3) | copy-done | bytes 524312
  47.4 0.0 copy-start.5
  47.4 1.0 %copy-done.5 = bf16[2,128,1024]{2,1,0:T(8,128)(2,1)S(1)} copy-done((bf16[2,128,1024]{2,1,0:T(8,128)(2,1)S(1)}, bf16[2,128,1024]{2,1,0:T(8,128)(2,1)}, u32[]{:S(2)}) %copy-start.5) | copy-done | bytes 524312
  48.5 0.0 copy-start.7
  48.5 1.0 %copy-done.7 = bf16[2,128,1024]{2,1,0:T(8,128)(2,1)S(1)} copy-done((bf16[2,128,1024]{2,1,0:T(8,128)(2,1)S(1)}, bf16[2,128,1024]{2,1,0:T(8,128)(2,1)}, u32[]{:S(2)}) %copy-start.7) | copy-done | bytes 524312
  49.5 11.4 %near_days.1.refs_7_ = f32[3,129,32,128]{3,2,1,0:T(8,128)} custom-call(s32[4]{0:T(128)S(1)} %pad_add_fusion.win, bf16[2,128,1024]{2,1,0:T(8,128)(2,1)S(1)} %copy-done.3, bf16[4,128,1024]{2,1,0:T(8,128)(2,1)} %collective-permute-done.9.refs_1_, bf16[2,128,1024]{2,1,0:T(8,128)(2,1)S(1)} %copy-done.7, bf16[2,128,1024]{2,1,0:T(8,128)(2,1)S(1)} %copy-done.5), custom_call_target="tpu_custom_call" | custom-call | flops 1048576 | bytes 65536 | tf_op jit(solution)/shard_map/near_days/pallas_call | solution.py:267
  60.9 0.0 collective-permute-done.8.refs_6_.refs_7_
  61.0 8.2 %collective-permute-done.7.refs_5_.refs_6_ = bf16[2,128,1024]{2,1,0:T(8,128)(2,1)} collective-permute-done((bf16[2,128,1024]{2,1,0:T(8,128)(2,1)}, bf16[2,128,1024]{2,1,0:T(8,128)(2,1)}, u32[]{:S(2)}, u32[]{:S(2)}) %collective-permute-start.7) | collective-permute-done | bytes 524320 | tf_op jit(solution)/shard_map/ppermute | solution.py:307
  69.2 0.0 collective-permute-done.6.refs_4_.refs_3_
  69.2 0.0 collective-permute-done.5.refs_3_.refs_1_.refs_2_
  69.2 0.0 copy-done.1
  69.2 1.3 %pair_far.1 = bf16[12,128,1024]{2,1,0:T(8,128)(2,1)S(1)} custom-call(s32[1]{0:T(128)} %bitcast.2.flag, bf16[2,128,1024]{2,1,0:T(8,128)(2,1)S(1)} %collective-permute-done.3.refs_0_, bf16[2,128,1024]{2,1,0:T(8,128)(2,1)S(1)} %collective-permute-done.2.refs_1_.refs_2_.refs_3_, bf16[2,128,1024]{2,1,0:T(8,128)(2,1)S(1)} %copy-done.1, ...), custom_call_target="tpu_custom_call" | custom-call | tf_op jit(solution)/shard_map/pair_far/pallas_call | solution.py:63
  70.5 0.7 collective-permute-start.10
  71.1 11.5 %far_days_one.1.refs_8_ = f32[3,129,32,128]{3,2,1,0:T(8,128)} custom-call(s32[4]{0:T(128)S(1)} %pad_add_fusion.win, bf16[2,128,1024]{2,1,0:T(8,128)(2,1)S(1)} %collective-permute-done.3.refs_0_, bf16[4,128,1024]{2,1,0:T(8,128)(2,1)S(1)} %collective-permute-done.5.refs_3_.refs_1_.refs_2_, ...), custom_call_target="tpu_custom_call", output_to_operand_aliasing={{}: (8, {})} | custom-call | flops 1048576 | bytes 65536 | tf_op jit(solution)/shard_map/far_days_one/pallas_call | solution.py:267
  82.6 0.0 collective-permute-done.10.refs_1_
  82.6 20.0 %far_days_rest.1 = f32[3,129,32,128]{3,2,1,0:T(8,128)} custom-call(s32[4]{0:T(128)S(1)} %pad_add_fusion.win, bf16[2,128,1024]{2,1,0:T(8,128)(2,1)S(1)} %collective-permute-done.3.refs_0_, bf16[12,128,1024]{2,1,0:T(8,128)(2,1)S(1)} %collective-permute-done.10.refs_1_, ...), custom_call_target="tpu_custom_call", output_to_operand_aliasing={{}: (9, {})} | custom-call | flops 1048576 | bytes 65536 | tf_op jit(solution)/shard_map/far_days_rest/pallas_call | solution.py:267
Async XLA Ops:
  2.2 17.3 %collective-permute-start.4 = (bf16[2,128,1024]{2,1,0:T(8,128)(2,1)}, bf16[2,128,1024]{2,1,0:T(8,128)(2,1)S(1)}, u32[]{:S(2)}, u32[]{:S(2)}) collective-permute-start(bf16[2,128,1024]{2,1,0:T(8,128)(2,1)} %whiten.1.refs_0_), channel_id=1, source_target_pairs={{4,0},{5,1},{6,2},{7,3},{8,4},{9,5},{10,6},{11,7},{12,8},{13,9},{1... | collective-permute-start | bytes 1572872 | tf_op jit(solution)/shard_map/ppermute | solution.py:307
  7.6 12.8 %collective-permute-start.3 = (bf16[2,128,1024]{2,1,0:T(8,128)(2,1)}, bf16[2,128,1024]{2,1,0:T(8,128)(2,1)S(1)}, u32[]{:S(2)}, u32[]{:S(2)}) collective-permute-start(bf16[2,128,1024]{2,1,0:T(8,128)(2,1)} %whiten.1.refs_0_), channel_id=1, source_target_pairs={{0,32},{32,64},{64,96},{96,0},{1,33},{33,65},{65,97},{97,1},{2,34}... | collective-permute-start | bytes 1572872 | tf_op jit(solution)/shard_map/ppermute | solution.py:307
  7.8 13.9 %collective-permute-start.2 = (bf16[2,128,1024]{2,1,0:T(8,128)(2,1)}, bf16[2,128,1024]{2,1,0:T(8,128)(2,1)S(1)}, u32[]{:S(2)}, u32[]{:S(2)}) collective-permute-start(bf16[2,128,1024]{2,1,0:T(8,128)(2,1)} %whiten.1.refs_0_), channel_id=1, source_target_pairs={{0,96},{32,0},{64,32},{96,64},{1,97},{33,1},{65,33},{97,65},{2,98}... | collective-permute-start | bytes 1572872 | tf_op jit(solution)/shard_map/ppermute | solution.py:307
  9.1 24.0 %collective-permute-start.1 = (bf16[2,128,1024]{2,1,0:T(8,128)(2,1)}, bf16[2,128,1024]{2,1,0:T(8,128)(2,1)S(1)}, u32[]{:S(2)}, u32[]{:S(2)}) collective-permute-start(bf16[2,128,1024]{2,1,0:T(8,128)(2,1)} %whiten.1.refs_0_), channel_id=1, source_target_pairs={{2,0},{3,1},{4,2},{5,3},{6,4},{7,5},{8,6},{9,7},{10,8},{11,9},{12,... | collective-permute-start | bytes 1572872 | tf_op jit(solution)/shard_map/ppermute | solution.py:307
  11.4 21.7 %collective-permute-start = (bf16[2,128,1024]{2,1,0:T(8,128)(2,1)}, bf16[2,128,1024]{2,1,0:T(8,128)(2,1)S(1)}, u32[]{:S(2)}, u32[]{:S(2)}) collective-permute-start(bf16[2,128,1024]{2,1,0:T(8,128)(2,1)} %whiten.1.refs_0_), channel_id=1, source_target_pairs={{0,64},{32,96},{64,0},{96,32},{1,65},{33,97},{65,1},{97,33},{2,66}... | collective-permute-start | bytes 1572872 | tf_op jit(solution)/shard_map/ppermute | solution.py:307
  19.5 18.3 %copy-start.4 = (bf16[2,128,1024]{2,1,0:T(8,128)(2,1)}, bf16[2,128,1024]{2,1,0:T(8,128)(2,1)S(1)}, u32[]{:S(2)}) copy-start(bf16[2,128,1024]{2,1,0:T(8,128)(2,1)S(1)} %collective-permute-done.4.refs_2_.refs_3_) | copy-start | bytes 1572868
  33.1 4.7 %copy-start.6 = (bf16[2,128,1024]{2,1,0:T(8,128)(2,1)}, bf16[2,128,1024]{2,1,0:T(8,128)(2,1)S(1)}, u32[]{:S(2)}) copy-start(bf16[2,128,1024]{2,1,0:T(8,128)(2,1)S(1)} %collective-permute-done.1.refs_1_.refs_2_) | copy-start | bytes 1572868
  33.1 4.7 %copy-start = (bf16[2,128,1024]{2,1,0:T(8,128)(2,1)}, bf16[2,128,1024]{2,1,0:T(8,128)(2,1)S(1)}, u32[]{:S(2)}) copy-start(bf16[2,128,1024]{2,1,0:T(8,128)(2,1)S(1)} %collective-permute-done.refs_2_.refs_4_.refs_5_) | copy-start | bytes 1572868
  33.1 1.4 %copy-start.2 = (bf16[2,128,1024]{2,1,0:T(8,128)(2,1)S(1)}, bf16[2,128,1024]{2,1,0:T(8,128)(2,1)}, u32[]{:S(2)}) copy-start(bf16[2,128,1024]{2,1,0:T(8,128)(2,1)} %whiten.1.refs_0_) | copy-start | bytes 1572868
  36.0 10.3 %collective-permute-start.9 = (bf16[4,128,1024]{2,1,0:T(8,128)(2,1)}, bf16[4,128,1024]{2,1,0:T(8,128)(2,1)}, u32[]{:S(2)}, u32[]{:S(2)}) collective-permute-start(bf16[4,128,1024]{2,1,0:T(8,128)(2,1)} %get-tuple-element.23), channel_id=1, source_target_pairs={{0,1},{1,0},{2,3},{3,2},{4,5},{5,4},{6,7},{7,6},{8,9},{9,8},{10,11... | collective-permute-start | bytes 3145736 | tf_op jit(solution)/shard_map/ppermute | solution.py:312
  37.9 31.3 %collective-permute-start.6 = (bf16[4,128,1024]{2,1,0:T(8,128)(2,1)}, bf16[4,128,1024]{2,1,0:T(8,128)(2,1)S(1)}, u32[]{:S(2)}, u32[]{:S(2)}) collective-permute-start(bf16[4,128,1024]{2,1,0:T(8,128)(2,1)} %get-tuple-element.22), channel_id=1, source_target_pairs={{0,96},{32,0},{64,32},{96,64},{1,97},{33,1},{65,33},{97,65},{2,98}... | collective-permute-start | bytes 3145736 | tf_op jit(solution)/shard_map/ppermute | solution.py:307
  37.9 31.2 %collective-permute-start.5 = (bf16[4,128,1024]{2,1,0:T(8,128)(2,1)}, bf16[4,128,1024]{2,1,0:T(8,128)(2,1)S(1)}, u32[]{:S(2)}, u32[]{:S(2)}) collective-permute-start(bf16[4,128,1024]{2,1,0:T(8,128)(2,1)} %get-tuple-element.22), channel_id=1, source_target_pairs={{0,32},{32,64},{64,96},{96,0},{1,33},{33,65},{65,97},{97,1},{2,34}... | collective-permute-start | bytes 3145736 | tf_op jit(solution)/shard_map/ppermute | solution.py:307
  40.6 20.4 %collective-permute-start.8 = (bf16[2,128,1024]{2,1,0:T(8,128)(2,1)}, bf16[2,128,1024]{2,1,0:T(8,128)(2,1)}, u32[]{:S(2)}, u32[]{:S(2)}) collective-permute-start(bf16[2,128,1024]{2,1,0:T(8,128)(2,1)} %copy-done), channel_id=1, source_target_pairs={{4,0},{5,1},{6,2},{7,3},{8,4},{9,5},{10,6},{11,7},{12,8},{13,9},{1... | collective-permute-start | bytes 1572872 | tf_op jit(solution)/shard_map/ppermute | solution.py:307
  42.5 26.6 %collective-permute-start.7 = (bf16[2,128,1024]{2,1,0:T(8,128)(2,1)}, bf16[2,128,1024]{2,1,0:T(8,128)(2,1)}, u32[]{:S(2)}, u32[]{:S(2)}) collective-permute-start(bf16[2,128,1024]{2,1,0:T(8,128)(2,1)} %copy-done), channel_id=1, source_target_pairs={{2,0},{3,1},{4,2},{5,3},{6,4},{7,5},{8,6},{9,7},{10,8},{11,9},{12,... | collective-permute-start | bytes 1572872 | tf_op jit(solution)/shard_map/ppermute | solution.py:307
  45.6 23.6 %copy-start.1 = (bf16[2,128,1024]{2,1,0:T(8,128)(2,1)S(1)}, bf16[2,128,1024]{2,1,0:T(8,128)(2,1)}, u32[]{:S(2)}) copy-start(bf16[2,128,1024]{2,1,0:T(8,128)(2,1)} %copy-done) | copy-start | bytes 1572868
  46.4 1.0 %copy-start.3 = (bf16[2,128,1024]{2,1,0:T(8,128)(2,1)S(1)}, bf16[2,128,1024]{2,1,0:T(8,128)(2,1)}, u32[]{:S(2)}) copy-start(bf16[2,128,1024]{2,1,0:T(8,128)(2,1)} %whiten.1.refs_0_) | copy-start | bytes 1572868
  47.4 1.0 %copy-start.5 = (bf16[2,128,1024]{2,1,0:T(8,128)(2,1)S(1)}, bf16[2,128,1024]{2,1,0:T(8,128)(2,1)}, u32[]{:S(2)}) copy-start(bf16[2,128,1024]{2,1,0:T(8,128)(2,1)} %copy-done.4) | copy-start | bytes 1572868
  48.5 1.0 %copy-start.7 = (bf16[2,128,1024]{2,1,0:T(8,128)(2,1)S(1)}, bf16[2,128,1024]{2,1,0:T(8,128)(2,1)}, u32[]{:S(2)}) copy-start(bf16[2,128,1024]{2,1,0:T(8,128)(2,1)} %copy-done.6) | copy-start | bytes 1572868
  70.5 12.2 %collective-permute-start.10 = (bf16[12,128,1024]{2,1,0:T(8,128)(2,1)S(1)}, bf16[12,128,1024]{2,1,0:T(8,128)(2,1)S(1)}, u32[]{:S(2)}, u32[]{:S(2)}) collective-permute-start(bf16[12,128,1024]{2,1,0:T(8,128)(2,1)S(1)} %pair_far.1), channel_id=1, source_target_pairs={{0,1},{1,0},{2,3},{3,2},{4,5},{5,4},{6,7},{7,6},{8,9},{9,8},{10,11... | collective-permute-start | bytes 9437192 | tf_op jit(solution)/shard_map/ppermute | solution.py:312

commit v4 on v3

--- a/solution.py
+++ b/solution.py
@@ -151,7 +151,7 @@
             for k in range(TILES_DEV):
                 pl.when(jnp.logical_not(lives[k]))(copy_zero(k).start)
 
-        gap = jnp.zeros((rows, MAXLAG), BF)
+        gap = jnp.zeros((rows, 2 * MAXLAG), BF)
         gap_b = jnp.zeros((BW, MAXLAG), BF)
         for s in range(sets):
             copy_left(s).wait()
@@ -169,10 +169,10 @@
 
         def make_right(s, seat):
             rights[s][0:BW, :] = jnp.concatenate(
-                [p for d in range(days) for p in (gap_b, braw[seat, s, d])], 1
+                [p for d in range(days) for p in (gap_b, braw[seat, s, d], gap_b)], 1
             )
             rights[s][BW : 2 * BW, :] = jnp.concatenate(
-                [p for d in range(days) for p in (braw[seat, s, d], gap_b)], 1
+                [p for d in range(days) for p in (braw[seat, s, d], gap_b, gap_b)], 1
             )
 
         def work(k, seat, with_shift):
@@ -242,7 +242,7 @@
 def correlate(sets, part, slots, scalars, total, rows, norm, name):
     count = len(sets)
     days = 2
-    span = days * (SAMPLES + MAXLAG)
+    span = days * (SAMPLES + 2 * MAXLAG)
     operands = []
 
     def place(block):
@@ -290,7 +290,7 @@
         ),
         out_shape=jax.ShapeDtypeStruct(tile, jnp.float32),
         input_output_aliases=aliases,
-        compiler_params=pltpu.CompilerParams(vmem_limit_bytes=(46 if slots * count > 3 else 32) << 20),
+        compiler_params=pltpu.CompilerParams(vmem_limit_bytes=(48 if slots * count > 3 else 32) << 20),
         cost_estimate=pl.CostEstimate(
             flops=1 << 20, bytes_accessed=1 << 16, transcendentals=0
         ),

time: 103 us -> 105 us (1.019)
  local copies, waits for them, and re-layouts: 4.56 us -> 6.2 us
    unnamed x16 -> x18, local copies, waits for them, and re-layouts: 4.56 us -> 6.2 us
where the time goes in v4:
time: 105 us
  Pallas kernels  48.1 us (46%)
  waiting for transfers between devices  28.7 us (27%)
  starting transfers between devices  20.6 us (20%)
  local copies, waits for them, and re-layouts  6.2 us (6%)
    pallas_call x3, Pallas kernels, correlate(): pl.pallas_call(functools.partial(correlate_kernel, places, arrays, part,...  43.2 us
    ppermute x9, waiting for transfers between devices, moved(): return lax.ppermute(array, axis, pairs)  28.7 us
    ppermute x9, starting transfers between devices, moved(): return lax.ppermute(array, axis, pairs)  18.2 us
    unnamed x18, local copies, waits for them, and re-layouts  6.2 us
    pallas_call x2, Pallas kernels, gather(): pl.pallas_call(functools.partial(gather_kernel, (len(arrays), even, odd))...  2.79 us
    ppermute x2, starting transfers between devices, swapped(): return lax.ppermute(array, 'chan', [(i, i ^ 1) for i in range(devices)])  2.49 us
    pallas_call x1, Pallas kernels, whiten(): pl.pallas_call(whiten_kernel, in_specs=[pl.BlockSpec(memory_space=pltpu.V...  2.17 us
  transfers between devices with their start and end apart: 11, of which 5 were waited for; matrix products, arithmetic and copies ran while one was open for 1% of the time, Pallas kernels for 22%

profile of v4, /device:TPU:15, one launch (start us, length us, event | category | flops | bytes accessed | tf_op | source)
XLA Modules:
  0.0 104.8 jit_solution(13303756043782571794)
XLA Ops:
  0.0 2.2 %whiten.1.refs_0_ = bf16[2,128,1024]{2,1,0:T(8,128)(2,1)} custom-call(bf16[2,128,1024]{2,1,0:T(8,128)(2,1)} %raw_ref.1), custom_call_target="tpu_custom_call" | custom-call | flops 2097152 | bytes 1048576 | tf_op jit(solution)/shard_map/whiten/pallas_call | solution.py:29
  2.2 5.4 %collective-permute-start.4 = (bf16[2,128,1024]{2,1,0:T(8,128)(2,1)}, bf16[2,128,1024]{2,1,0:T(8,128)(2,1)S(1)}, u32[]{:S(2)}, u32[]{:S(2)}) collective-permute-start(bf16[2,128,1024]{2,1,0:T(8,128)(2,1)} %whiten.1.refs_0_), channel_id=1, source_target_pairs={{4,0},{5,1},{6,2},{7,3},{8,4},{9,5},{10,6},{11,7},{12,8},{13,9},{1... | collective-permute-start | bytes 1572872 | tf_op jit(solution)/shard_map/ppermute | solution.py:307
  7.6 0.3 collective-permute-start.3
  7.8 1.3 %collective-permute-start.2 = (bf16[2,128,1024]{2,1,0:T(8,128)(2,1)}, bf16[2,128,1024]{2,1,0:T(8,128)(2,1)S(1)}, u32[]{:S(2)}, u32[]{:S(2)}) collective-permute-start(bf16[2,128,1024]{2,1,0:T(8,128)(2,1)} %whiten.1.refs_0_), channel_id=1, source_target_pairs={{0,96},{32,0},{64,32},{96,64},{1,97},{33,1},{65,33},{97,65},{2,98}... | collective-permute-start | bytes 1572872 | tf_op jit(solution)/shard_map/ppermute | solution.py:307
  9.1 2.3 %collective-permute-start.1 = (bf16[2,128,1024]{2,1,0:T(8,128)(2,1)}, bf16[2,128,1024]{2,1,0:T(8,128)(2,1)S(1)}, u32[]{:S(2)}, u32[]{:S(2)}) collective-permute-start(bf16[2,128,1024]{2,1,0:T(8,128)(2,1)} %whiten.1.refs_0_), channel_id=1, source_target_pairs={{2,0},{3,1},{4,2},{5,3},{6,4},{7,5},{8,6},{9,7},{10,8},{11,9},{12,... | collective-permute-start | bytes 1572872 | tf_op jit(solution)/shard_map/ppermute | solution.py:307
  11.4 1.2 %collective-permute-start = (bf16[2,128,1024]{2,1,0:T(8,128)(2,1)}, bf16[2,128,1024]{2,1,0:T(8,128)(2,1)S(1)}, u32[]{:S(2)}, u32[]{:S(2)}) collective-permute-start(bf16[2,128,1024]{2,1,0:T(8,128)(2,1)} %whiten.1.refs_0_), channel_id=1, source_target_pairs={{0,64},{32,96},{64,0},{96,32},{1,65},{33,97},{65,1},{97,33},{2,66}... | collective-permute-start | bytes 1572872 | tf_op jit(solution)/shard_map/ppermute | solution.py:307
  12.6 6.9 %collective-permute-done.4.refs_2_.refs_3_ = bf16[2,128,1024]{2,1,0:T(8,128)(2,1)S(1)} collective-permute-done((bf16[2,128,1024]{2,1,0:T(8,128)(2,1)}, bf16[2,128,1024]{2,1,0:T(8,128)(2,1)S(1)}, u32[]{:S(2)}, u32[]{:S(2)}) %collective-permute-start.4) | collective-permute-done | bytes 524320 | tf_op jit(solution)/shard_map/ppermute | solution.py:307
  19.5 0.0 copy-start.4
  19.5 0.8 collective-permute-done.3.refs_0_
  20.3 1.4 %collective-permute-done.2.refs_1_.refs_2_.refs_3_ = bf16[2,128,1024]{2,1,0:T(8,128)(2,1)S(1)} collective-permute-done((bf16[2,128,1024]{2,1,0:T(8,128)(2,1)}, bf16[2,128,1024]{2,1,0:T(8,128)(2,1)S(1)}, u32[]{:S(2)}, u32[]{:S(2)}) %collective-permute-start.2) | collective-permute-done | bytes 524320 | tf_op jit(solution)/shard_map/ppermute | solution.py:307
  21.7 11.4 %collective-permute-done.1.refs_1_.refs_2_ = bf16[2,128,1024]{2,1,0:T(8,128)(2,1)S(1)} collective-permute-done((bf16[2,128,1024]{2,1,0:T(8,128)(2,1)}, bf16[2,128,1024]{2,1,0:T(8,128)(2,1)S(1)}, u32[]{:S(2)}, u32[]{:S(2)}) %collective-permute-start.1) | collective-permute-done | bytes 524320 | tf_op jit(solution)/shard_map/ppermute | solution.py:307
  33.1 0.0 copy-start.6
  33.1 0.0 collective-permute-done.refs_2_.refs_4_.refs_5_
  33.1 0.0 copy-start
  33.1 0.0 copy-start.2
  33.1 1.4 %copy-done.2 = bf16[2,128,1024]{2,1,0:T(8,128)(2,1)S(1)} copy-done((bf16[2,128,1024]{2,1,0:T(8,128)(2,1)S(1)}, bf16[2,128,1024]{2,1,0:T(8,128)(2,1)}, u32[]{:S(2)}) %copy-start.2) | copy-done | bytes 524312
  34.5 1.5 %pair_near.1 = (bf16[4,128,1024]{2,1,0:T(8,128)(2,1)}, bf16[4,128,1024]{2,1,0:T(8,128)(2,1)}) custom-call(s32[1]{0:T(128)} %bitcast.2.flag, bf16[2,128,1024]{2,1,0:T(8,128)(2,1)S(1)} %copy-done.2, bf16[2,128,1024]{2,1,0:T(8,128)(2,1)S(1)} %collective-permute-done.1.refs_1_.refs_2_, bf16[2,128,1024]{2,1,0:T(8,128)(2,1)S(1)} %collective-permute-done.4.refs_2_.refs_3_), custom_call_target="tpu_custom_call" | custom-call | tf_op jit(solution)/shard_map/pair_near/pallas_call | solution.py:63
  36.0 1.8 %collective-permute-start.9 = (bf16[4,128,1024]{2,1,0:T(8,128)(2,1)}, bf16[4,128,1024]{2,1,0:T(8,128)(2,1)}, u32[]{:S(2)}, u32[]{:S(2)}) collective-permute-start(bf16[4,128,1024]{2,1,0:T(8,128)(2,1)} %get-tuple-element.23), channel_id=1, source_target_pairs={{0,1},{1,0},{2,3},{3,2},{4,5},{5,4},{6,7},{7,6},{8,9},{9,8},{10,11... | collective-permute-start | bytes 3145736 | tf_op jit(solution)/shard_map/ppermute | solution.py:312
  37.9 0.0 copy-done.4
  37.9 0.0 copy-done
  37.9 0.0 copy-done.6
  37.9 0.1 collective-permute-start.6
  37.9 2.7 %collective-permute-start.5 = (bf16[4,128,1024]{2,1,0:T(8,128)(2,1)}, bf16[4,128,1024]{2,1,0:T(8,128)(2,1)S(1)}, u32[]{:S(2)}, u32[]{:S(2)}) collective-permute-start(bf16[4,128,1024]{2,1,0:T(8,128)(2,1)} %get-tuple-element.22), channel_id=1, source_target_pairs={{0,32},{32,64},{64,96},{96,0},{1,33},{33,65},{65,97},{97,1},{2,34}... | collective-permute-start | bytes 3145736 | tf_op jit(solution)/shard_map/ppermute | solution.py:307
  40.6 1.9 %collective-permute-start.8 = (bf16[2,128,1024]{2,1,0:T(8,128)(2,1)}, bf16[2,128,1024]{2,1,0:T(8,128)(2,1)}, u32[]{:S(2)}, u32[]{:S(2)}) collective-permute-start(bf16[2,128,1024]{2,1,0:T(8,128)(2,1)} %copy-done), channel_id=1, source_target_pairs={{4,0},{5,1},{6,2},{7,3},{8,4},{9,5},{10,6},{11,7},{12,8},{13,9},{1... | collective-permute-start | bytes 1572872 | tf_op jit(solution)/shard_map/ppermute | solution.py:307
  42.5 3.1 %collective-permute-start.7 = (bf16[2,128,1024]{2,1,0:T(8,128)(2,1)}, bf16[2,128,1024]{2,1,0:T(8,128)(2,1)}, u32[]{:S(2)}, u32[]{:S(2)}) collective-permute-start(bf16[2,128,1024]{2,1,0:T(8,128)(2,1)} %copy-done), channel_id=1, source_target_pairs={{2,0},{3,1},{4,2},{5,3},{6,4},{7,5},{8,6},{9,7},{10,8},{11,9},{12,... | collective-permute-start | bytes 1572872 | tf_op jit(solution)/shard_map/ppermute | solution.py:307
  45.6 0.0 copy-start.1
  45.6 0.8 pad_add_fusion.win
  46.4 0.0 collective-permute-done.9.refs_1_
  46.4 0.0 copy-start.3
  46.4 1.0 copy-done.3
  47.4 0.0 copy-start.5
  47.4 1.0 copy-done.5
  48.5 0.0 copy-start.7
  48.5 1.0 copy-done.7
  49.5 11.4 %near_days.1.refs_7_ = f32[3,129,32,128]{3,2,1,0:T(8,128)} custom-call(s32[4]{0:T(128)S(1)} %pad_add_fusion.win, bf16[2,128,1024]{2,1,0:T(8,128)(2,1)S(1)} %copy-done.3, bf16[4,128,1024]{2,1,0:T(8,128)(2,1)} %collective-permute-done.9.refs_1_, bf16[2,128,1024]{2,1,0:T(8,128)(2,1)S(1)} %copy-done.7, bf16[2,128,1024]{2,1,0:T(8,128)(2,1)S(1)} %copy-done.5), custom_call_target="tpu_custom_call" | custom-call | flops 1048576 | bytes 65536 | tf_op jit(solution)/shard_map/near_days/pallas_call | solution.py:267
  60.9 0.0 collective-permute-done.8.refs_6_.refs_7_
  60.9 8.2 %collective-permute-done.7.refs_5_.refs_6_ = bf16[2,128,1024]{2,1,0:T(8,128)(2,1)} collective-permute-done((bf16[2,128,1024]{2,1,0:T(8,128)(2,1)}, bf16[2,128,1024]{2,1,0:T(8,128)(2,1)}, u32[]{:S(2)}, u32[]{:S(2)}) %collective-permute-start.7) | collective-permute-done | bytes 524320 | tf_op jit(solution)/shard_map/ppermute | solution.py:307
  69.2 0.0 collective-permute-done.6.refs_4_.refs_3_
  69.2 0.0 collective-permute-done.5.refs_3_.refs_1_.refs_2_
  69.2 0.0 copy-done.1
  69.2 1.3 %pair_far.1 = bf16[12,128,1024]{2,1,0:T(8,128)(2,1)S(1)} custom-call(s32[1]{0:T(128)} %bitcast.2.flag, bf16[2,128,1024]{2,1,0:T(8,128)(2,1)S(1)} %collective-permute-done.3.refs_0_, bf16[2,128,1024]{2,1,0:T(8,128)(2,1)S(1)} %collective-permute-done.2.refs_1_.refs_2_.refs_3_, bf16[2,128,1024]{2,1,0:T(8,128)(2,1)S(1)} %copy-done.1, ...), custom_call_target="tpu_custom_call" | custom-call | tf_op jit(solution)/shard_map/pair_far/pallas_call | solution.py:63
  70.5 0.7 collective-permute-start.10
  71.1 11.3 %far_days_one.1.refs_8_ = f32[3,129,32,128]{3,2,1,0:T(8,128)} custom-call(s32[4]{0:T(128)S(1)} %pad_add_fusion.win, bf16[2,128,1024]{2,1,0:T(8,128)(2,1)S(1)} %collective-permute-done.3.refs_0_, bf16[4,128,1024]{2,1,0:T(8,128)(2,1)S(1)} %collective-permute-done.5.refs_3_.refs_1_.refs_2_, ...), custom_call_target="tpu_custom_call", output_to_operand_aliasing={{}: (8, {})} | custom-call | flops 1048576 | bytes 65536 | tf_op jit(solution)/shard_map/far_days_one/pallas_call | solution.py:267
  82.5 0.0 collective-permute-done.10.refs_1_
  82.5 0.0 copy-start.8
  82.5 1.6 %copy-done.8 = bf16[12,128,1024]{2,1,0:T(8,128)(2,1)} copy-done((bf16[12,128,1024]{2,1,0:T(8,128)(2,1)}, bf16[12,128,1024]{2,1,0:T(8,128)(2,1)S(1)}, u32[]{:S(2)}) %copy-start.8) | copy-done | bytes 3145752
  84.1 20.4 %far_days_rest.1 = f32[3,129,32,128]{3,2,1,0:T(8,128)} custom-call(s32[4]{0:T(128)S(1)} %pad_add_fusion.win, bf16[2,128,1024]{2,1,0:T(8,128)(2,1)S(1)} %collective-permute-done.3.refs_0_, bf16[12,128,1024]{2,1,0:T(8,128)(2,1)} %copy-done.8, bf16[4,128,1024]{2,1,0:T(8,128)(2,1)S(1)} %collective-permute-done.5.refs_3_.refs_1_.refs_2_, ...), custom_call_target="tpu_custom_call", output_to_operand_aliasing={{}: (9, {})} | custom-call | flops 1048576 | bytes 65536 | tf_op jit(solution)/shard_map/far_days_rest/pallas_call | solution.py:267
Async XLA Ops:
  2.2 17.3 %collective-permute-start.4 = (bf16[2,128,1024]{2,1,0:T(8,128)(2,1)}, bf16[2,128,1024]{2,1,0:T(8,128)(2,1)S(1)}, u32[]{:S(2)}, u32[]{:S(2)}) collective-permute-start(bf16[2,128,1024]{2,1,0:T(8,128)(2,1)} %whiten.1.refs_0_), channel_id=1, source_target_pairs={{4,0},{5,1},{6,2},{7,3},{8,4},{9,5},{10,6},{11,7},{12,8},{13,9},{1... | collective-permute-start | bytes 1572872 | tf_op jit(solution)/shard_map/ppermute | solution.py:307
  7.6 12.8 %collective-permute-start.3 = (bf16[2,128,1024]{2,1,0:T(8,128)(2,1)}, bf16[2,128,1024]{2,1,0:T(8,128)(2,1)S(1)}, u32[]{:S(2)}, u32[]{:S(2)}) collective-permute-start(bf16[2,128,1024]{2,1,0:T(8,128)(2,1)} %whiten.1.refs_0_), channel_id=1, source_target_pairs={{0,32},{32,64},{64,96},{96,0},{1,33},{33,65},{65,97},{97,1},{2,34}... | collective-permute-start | bytes 1572872 | tf_op jit(solution)/shard_map/ppermute | solution.py:307
  7.8 13.9 %collective-permute-start.2 = (bf16[2,128,1024]{2,1,0:T(8,128)(2,1)}, bf16[2,128,1024]{2,1,0:T(8,128)(2,1)S(1)}, u32[]{:S(2)}, u32[]{:S(2)}) collective-permute-start(bf16[2,128,1024]{2,1,0:T(8,128)(2,1)} %whiten.1.refs_0_), channel_id=1, source_target_pairs={{0,96},{32,0},{64,32},{96,64},{1,97},{33,1},{65,33},{97,65},{2,98}... | collective-permute-start | bytes 1572872 | tf_op jit(solution)/shard_map/ppermute | solution.py:307
  9.1 24.0 %collective-permute-start.1 = (bf16[2,128,1024]{2,1,0:T(8,128)(2,1)}, bf16[2,128,1024]{2,1,0:T(8,128)(2,1)S(1)}, u32[]{:S(2)}, u32[]{:S(2)}) collective-permute-start(bf16[2,128,1024]{2,1,0:T(8,128)(2,1)} %whiten.1.refs_0_), channel_id=1, source_target_pairs={{2,0},{3,1},{4,2},{5,3},{6,4},{7,5},{8,6},{9,7},{10,8},{11,9},{12,... | collective-permute-start | bytes 1572872 | tf_op jit(solution)/shard_map/ppermute | solution.py:307
  11.4 21.7 %collective-permute-start = (bf16[2,128,1024]{2,1,0:T(8,128)(2,1)}, bf16[2,128,1024]{2,1,0:T(8,128)(2,1)S(1)}, u32[]{:S(2)}, u32[]{:S(2)}) collective-permute-start(bf16[2,128,1024]{2,1,0:T(8,128)(2,1)} %whiten.1.refs_0_), channel_id=1, source_target_pairs={{0,64},{32,96},{64,0},{96,32},{1,65},{33,97},{65,1},{97,33},{2,66}... | collective-permute-start | bytes 1572872 | tf_op jit(solution)/shard_map/ppermute | solution.py:307
  19.5 18.3 %copy-start.4 = (bf16[2,128,1024]{2,1,0:T(8,128)(2,1)}, bf16[2,128,1024]{2,1,0:T(8,128)(2,1)S(1)}, u32[]{:S(2)}) copy-start(bf16[2,128,1024]{2,1,0:T(8,128)(2,1)S(1)} %collective-permute-done.4.refs_2_.refs_3_) | copy-start | bytes 1572868
  33.1 4.7 %copy-start.6 = (bf16[2,128,1024]{2,1,0:T(8,128)(2,1)}, bf16[2,128,1024]{2,1,0:T(8,128)(2,1)S(1)}, u32[]{:S(2)}) copy-start(bf16[2,128,1024]{2,1,0:T(8,128)(2,1)S(1)} %collective-permute-done.1.refs_1_.refs_2_) | copy-start | bytes 1572868
  33.1 4.7 %copy-start = (bf16[2,128,1024]{2,1,0:T(8,128)(2,1)}, bf16[2,128,1024]{2,1,0:T(8,128)(2,1)S(1)}, u32[]{:S(2)}) copy-start(bf16[2,128,1024]{2,1,0:T(8,128)(2,1)S(1)} %collective-permute-done.refs_2_.refs_4_.refs_5_) | copy-start | bytes 1572868
  33.1 1.4 %copy-start.2 = (bf16[2,128,1024]{2,1,0:T(8,128)(2,1)S(1)}, bf16[2,128,1024]{2,1,0:T(8,128)(2,1)}, u32[]{:S(2)}) copy-start(bf16[2,128,1024]{2,1,0:T(8,128)(2,1)} %whiten.1.refs_0_) | copy-start | bytes 1572868
  36.0 10.3 %collective-permute-start.9 = (bf16[4,128,1024]{2,1,0:T(8,128)(2,1)}, bf16[4,128,1024]{2,1,0:T(8,128)(2,1)}, u32[]{:S(2)}, u32[]{:S(2)}) collective-permute-start(bf16[4,128,1024]{2,1,0:T(8,128)(2,1)} %get-tuple-element.23), channel_id=1, source_target_pairs={{0,1},{1,0},{2,3},{3,2},{4,5},{5,4},{6,7},{7,6},{8,9},{9,8},{10,11... | collective-permute-start | bytes 3145736 | tf_op jit(solution)/shard_map/ppermute | solution.py:312
  37.9 31.3 %collective-permute-start.6 = (bf16[4,128,1024]{2,1,0:T(8,128)(2,1)}, bf16[4,128,1024]{2,1,0:T(8,128)(2,1)S(1)}, u32[]{:S(2)}, u32[]{:S(2)}) collective-permute-start(bf16[4,128,1024]{2,1,0:T(8,128)(2,1)} %get-tuple-element.22), channel_id=1, source_target_pairs={{0,96},{32,0},{64,32},{96,64},{1,97},{33,1},{65,33},{97,65},{2,98}... | collective-permute-start | bytes 3145736 | tf_op jit(solution)/shard_map/ppermute | solution.py:307
  37.9 31.2 %collective-permute-start.5 = (bf16[4,128,1024]{2,1,0:T(8,128)(2,1)}, bf16[4,128,1024]{2,1,0:T(8,128)(2,1)S(1)}, u32[]{:S(2)}, u32[]{:S(2)}) collective-permute-start(bf16[4,128,1024]{2,1,0:T(8,128)(2,1)} %get-tuple-element.22), channel_id=1, source_target_pairs={{0,32},{32,64},{64,96},{96,0},{1,33},{33,65},{65,97},{97,1},{2,34}... | collective-permute-start | bytes 3145736 | tf_op jit(solution)/shard_map/ppermute | solution.py:307
  40.6 20.3 %collective-permute-start.8 = (bf16[2,128,1024]{2,1,0:T(8,128)(2,1)}, bf16[2,128,1024]{2,1,0:T(8,128)(2,1)}, u32[]{:S(2)}, u32[]{:S(2)}) collective-permute-start(bf16[2,128,1024]{2,1,0:T(8,128)(2,1)} %copy-done), channel_id=1, source_target_pairs={{4,0},{5,1},{6,2},{7,3},{8,4},{9,5},{10,6},{11,7},{12,8},{13,9},{1... | collective-permute-start | bytes 1572872 | tf_op jit(solution)/shard_map/ppermute | solution.py:307
  42.5 26.6 %collective-permute-start.7 = (bf16[2,128,1024]{2,1,0:T(8,128)(2,1)}, bf16[2,128,1024]{2,1,0:T(8,128)(2,1)}, u32[]{:S(2)}, u32[]{:S(2)}) collective-permute-start(bf16[2,128,1024]{2,1,0:T(8,128)(2,1)} %copy-done), channel_id=1, source_target_pairs={{2,0},{3,1},{4,2},{5,3},{6,4},{7,5},{8,6},{9,7},{10,8},{11,9},{12,... | collective-permute-start | bytes 1572872 | tf_op jit(solution)/shard_map/ppermute | solution.py:307
  45.6 23.6 %copy-start.1 = (bf16[2,128,1024]{2,1,0:T(8,128)(2,1)S(1)}, bf16[2,128,1024]{2,1,0:T(8,128)(2,1)}, u32[]{:S(2)}) copy-start(bf16[2,128,1024]{2,1,0:T(8,128)(2,1)} %copy-done) | copy-start | bytes 1572868
  46.4 1.0 copy-start.3
  47.4 1.0 copy-start.5
  48.5 1.0 copy-start.7
  70.5 12.0 %collective-permute-start.10 = (bf16[12,128,1024]{2,1,0:T(8,128)(2,1)S(1)}, bf16[12,128,1024]{2,1,0:T(8,128)(2,1)S(1)}, u32[]{:S(2)}, u32[]{:S(2)}) collective-permute-start(bf16[12,128,1024]{2,1,0:T(8,128)(2,1)S(1)} %pair_far.1), channel_id=1, source_target_pairs={{0,1},{1,0},{2,3},{3,2},{4,5},{5,4},{6,7},{7,6},{8,9},{9,8},{10,11... | collective-permute-start | bytes 9437192 | tf_op jit(solution)/shard_map/ppermute | solution.py:312
  82.5 1.7 %copy-start.8 = (bf16[12,128,1024]{2,1,0:T(8,128)(2,1)}, bf16[12,128,1024]{2,1,0:T(8,128)(2,1)S(1)}, u32[]{:S(2)}) copy-start(bf16[12,128,1024]{2,1,0:T(8,128)(2,1)S(1)} %collective-permute-done.10.refs_1_) | copy-start | bytes 9437188
